TPU v7x, 32 devices: a whole 2x2x4 slice. The times are simulated.
32 devices in a mesh: groups: 2 (over x), owners: 16 (over z, y, core).
Axes of the slice: x: 2, y: 2, z: 4, core: 2. Of those that a mesh axis runs over, the one named last changes fastest.
Arguments:
- embeddings: float32 [24576, 768], P(('groups', 'owners')), parts along dimension 0, may hold values from -1100 to 1100
- cluster_of: int32 [24576], P(('groups', 'owners')), parts along dimension 0, may hold values from 0 to 7, as said below
Outputs:
- best_score: float32 [24576], P(('groups', 'owners')), parts along dimension 0
There are 2 independent parts, one for each index of `groups`. A program takes and returns all parts, laid end to end along the dimension named above; each array names one. Nothing has to cross between parts.
Inputs may be any that keep to these rules, and one draw needn't show every extreme that they name: `cluster_of`: the rows of one ingest device (aligned blocks of 768 rows) hold at most 128 rows of any one cluster; in every draw some cluster has exactly 128 rows on every ingest device.
All inputs are finite; a program needn't handle non-finite values.
Results may differ from a plain program's by a relative error of at most 0.00043.
Values may be sent and summed in bfloat16 or wider, within the bound.
No kernel may reach another device: no remote copies, remote signals or barrier semaphores. Data moves between devices by JAX's collectives and lax.ppermute only.
A program may use at most 64 MiB of HBM per device.

v0:
```python
import jax
import jax.numpy as jnp
from jax import lax
from jax.sharding import PartitionSpec as P

SLOTS = 1024


floor_value = -4.0


def from_partner(value, axis, distance):
    mask = 2**distance
    pairs = [(source, source ^ mask) for source in range(lax.axis_size(axis))]
    return lax.ppermute(value, axis, pairs)


def scored(queries, key_block, key_live, start_row, skip_self):
    scores = jnp.einsum("id,jd->ij", queries, key_block, preferred_element_type=jnp.float32)
    keep_mask = key_live[None, :]
    if skip_self:
        query_index = start_row + jnp.arange(queries.shape[0], dtype=jnp.int32)
        key_index = jnp.arange(key_block.shape[0], dtype=jnp.int32)
        keep_mask = keep_mask & (query_index[:, None] != key_index[None, :])
    return jnp.where(keep_mask, scores, floor_value)


def occupied(own_block):
    return jnp.sum(jnp.square(own_block.astype(jnp.float32)), axis=1) > 0.5


def on_device(embeddings, cluster_of):
    owners = lax.axis_size("owners")
    rows_dev = embeddings.shape[0]
    feature_width = embeddings.shape[1]
    block_rows = SLOTS
    capacity = block_rows // owners
    clusters = owners // 2
    scale = lax.rsqrt(jnp.sum(embeddings * embeddings, axis=1, keepdims=True) + 1e-06)
    unit_rows = (embeddings * scale).astype(jnp.bfloat16)
    members = (cluster_of[:, None] == jnp.arange(clusters, dtype=jnp.int32)[None, :]).astype(
        jnp.int32
    )
    before = jnp.cumsum(members, axis=0) - members
    position = jnp.sum(before * members, axis=1)
    row_parity = position % 2
    slot_index = position // 2
    slot_place = (2 * cluster_of + row_parity) * capacity + slot_index
    row_ids = jnp.arange(rows_dev, dtype=jnp.int32)
    padded = jnp.concatenate([unit_rows, jnp.zeros((1, feature_width), jnp.bfloat16)], axis=0)
    row_table = jnp.full((owners * capacity,), rows_dev, jnp.int32).at[slot_place].set(row_ids)
    outgoing = jnp.take(padded, row_table, axis=0).reshape(owners, capacity, feature_width)
    incoming = lax.all_to_all(outgoing, "owners", split_axis=0, concat_axis=0, tiled=True)
    own_block = incoming.reshape(block_rows, feature_width)
    partner = from_partner(own_block, "owners", 0)
    live_rows = occupied(own_block)
    partner_live = occupied(partner)
    tile_rows = min(512, block_rows)
    tile_starts = jnp.arange(block_rows // tile_rows, dtype=jnp.int32) * tile_rows

    def both_tile(start_row):
        queries = lax.dynamic_slice_in_dim(own_block, start_row, tile_rows, 0)
        near_best = jnp.max(scored(queries, own_block, live_rows, start_row, True), axis=1)
        far_best = jnp.max(scored(queries, partner, partner_live, start_row, False), axis=1)
        return jnp.maximum(near_best, far_best)

    best_slots = lax.map(both_tile, tile_starts).reshape(block_rows)
    answers = lax.all_to_all(
        best_slots.reshape(owners, capacity), "owners", split_axis=0, concat_axis=0, tiled=True
    )
    returned_best = jnp.take(answers.reshape(owners * capacity), slot_place)
    return jnp.maximum(returned_best, -1.0)


def solution(mesh):
    placed = (P(("groups", "owners"), None), P(("groups", "owners")))
    return jax.shard_map(
        on_device, mesh=mesh, in_specs=placed, out_specs=P(("groups", "owners")), check_vma=False
    )
```

profile of v0, /device:TPU:0, one launch (start us, length us, event | category | flops | bytes accessed | tf_op | source)
XLA Modules:
  0.0 90.4 jit_solution(14174443653990615755)
XLA Ops:
  0.0 0.0 copy-start
  0.0 0.8 fusion.7
  0.8 1.7 %reduce-window.6 = s32[8,6,128]{2,0,1:T(8,128)S(1)} reduce-window(s32[8,6,128]{2,0,1:T(8,128)S(1)} %fusion.7, s32[]{:T(128)} %constant.78.clone.1), window={size=1x1x128 pad=0_0x0_0x127_0}, to_apply=%region_0.0 | reduce-window | flops 780288 | bytes 49156 | tf_op jit(solution)/shard_map/reduce-window
  2.5 0.1 slice.12
  2.6 0.1 copy.7
  2.7 0.2 reduce-window.9
  2.9 0.1 copy.8
  3.0 0.8 fusion.6
  3.8 0.7 compare_select_fusion.1
  4.5 3.4 %scatter_custom_fusion = s32[1024]{0:T(1024)S(1)} fusion(s32[768]{0:T(1024)S(1)} %compare_select_fusion.1, s32[768]{0:T(1024)S(1)} %iota.23, s32[]{:T(128)} %constant.86.clone.1), kind=kCustom, calls=%fused_computation.45 | custom fusion | bytes 4100 | tf_op jit(solution)/shard_map/scatter | solution.py:51
  7.9 1.9 %multiply_reduce_fusion.2 = f32[768]{0:T(1024)S(1)} fusion(f32[768,768]{1,0:T(8,128)} %param.4), kind=kLoop, calls=%fused_computation.15 | loop fusion | flops 1178880 | bytes 2362368 | tf_op jit(solution)/shard_map/reduce_sum | solution.py:39
  9.8 0.0 copy-done
  9.8 0.2 multiply_convert_fusion
  10.0 0.1 broadcast_in_dim.56
  10.1 0.1 concatenate.3
  10.2 4.0 %gather_fusion = bf16[1024,768]{1,0:T(8,128)(2,1)S(1)} fusion(bf16[769,768]{1,0:T(8,128)(2,1)S(1)} %concatenate.3, s32[1024]{0:T(1024)S(1)} %fusion.15), kind=kCustom, calls=%fused_computation | custom fusion | bytes 3149824 | tf_op jit(solution)/shard_map/jit(_take)/gather | solution.py:52
  14.2 0.2 broadcast_select_fusion
  14.4 43.3 %all_to_all.14 = bf16[16,64,768]{2,1,0:T(8,128)(2,1)S(1)} all-to-all(bf16[16,64,768]{2,1,0:T(8,128)(2,1)S(1)} %broadcast_select_fusion), channel_id=1, replica_groups=mesh['groups'=2,'owners'=16] {'owners'}, dimensions={0} | all-to-all | bytes 3145728 | tf_op jit(solution)/shard_map/all_to_all | solution.py:53
  57.7 0.8 collective-permute-start
  58.5 0.4 multiply_reduce_fusion.1
  58.8 0.1 gt.10
  58.9 2.6 %collective-permute-done = bf16[1024,768]{1,0:T(8,128)(2,1)S(1)} collective-permute-done((bf16[1024,768]{1,0:T(8,128)(2,1)S(1)}, bf16[1024,768]{1,0:T(8,128)(2,1)S(1)}, u32[]{:S(2)}, u32[]{:S(2)}) %collective-permute-start) | collective-permute-done | bytes 1572896 | tf_op jit(solution)/shard_map/ppermute | solution.py:15
  61.5 0.4 multiply_reduce_fusion
  61.9 11.7 %while.10 = (s32[]{:T(128)}, f32[2,512]{1,0:T(2,128)S(1)}, pred[1024]{0:T(1024)(128)(4,1)S(1)}, s32[2]{0:T(128)S(1)}, bf16[1024,768]{1,0:T(8,128)(2,1)S(1)}, /*i...) while((s32[]{:T(128)}, f32[2,512]{1,0:T(2,128)S(1)}, ...), condition=%wide.region_10.11_spmd, body=%wide.region_7.10_spmd.sunk | while | flops 1613758464 | bytes 4739235 | solution.py:67
  61.9 0.7 dynamic_slice.16
  64.6 0.7 iota_add_fusion.2
  65.3 1.2 %select_reduce_fusion.4 = f32[512]{0:T(512)S(1)} fusion(bf16[1024,768]{1,0:T(8,128)(2,1)S(1)} %get-tuple-element.124, s32[512]{0:T(512)S(1)} %iota_add_fusion.2, pred[1024]{0:T(1024)(128)(4,1)S(1)} %get-tuple-element.122, s32[]{:T(128)S(6)} %select_n.75), kind=kOutput, calls=%fused_computation.4.clone.1 | convolution fusion | flops 807403008 | bytes 2364420 | tf_op jit(solution)/shard_map/while/body/eval_jaxpr/id,jd->ij/dot_general | solution.py:19
  66.6 1.1 %select_reduce_fusion.5 = f32[512]{0:T(512)S(1)} fusion(bf16[1024,768]{1,0:T(8,128)(2,1)S(1)} %get-tuple-element.126, pred[1024]{0:T(1024)(128)(4,1)S(1)} %get-tuple-element.125, bf16[1024,768]{1,0:T(8,128)(2,1)S(1)} %get-tuple-element.124, s32[]{:T(128)S(6)} %select_n.75), kind=kOutput, calls=%fused_computation.3.clone.1 | convolution fusion | flops 806354432 | bytes 2362372 | tf_op jit(solution)/shard_map/while/body/eval_jaxpr/id,jd->ij/dot_general | solution.py:19
  67.8 0.7 dynamic_slice.16
  70.5 0.7 iota_add_fusion.2
  71.2 1.3 %select_reduce_fusion.4 = f32[512]{0:T(512)S(1)} fusion(bf16[1024,768]{1,0:T(8,128)(2,1)S(1)} %get-tuple-element.124, s32[512]{0:T(512)S(1)} %iota_add_fusion.2, pred[1024]{0:T(1024)(128)(4,1)S(1)} %get-tuple-element.122, s32[]{:T(128)S(6)} %select_n.75), kind=kOutput, calls=%fused_computation.4.clone.1 | convolution fusion | flops 807403008 | bytes 2364420 | tf_op jit(solution)/shard_map/while/body/eval_jaxpr/id,jd->ij/dot_general | solution.py:19
  72.5 1.1 %select_reduce_fusion.5 = f32[512]{0:T(512)S(1)} fusion(bf16[1024,768]{1,0:T(8,128)(2,1)S(1)} %get-tuple-element.126, pred[1024]{0:T(1024)(128)(4,1)S(1)} %get-tuple-element.125, bf16[1024,768]{1,0:T(8,128)(2,1)S(1)} %get-tuple-element.124, s32[]{:T(128)S(6)} %select_n.75), kind=kOutput, calls=%fused_computation.3.clone.1 | convolution fusion | flops 806354432 | bytes 2362372 | tf_op jit(solution)/shard_map/while/body/eval_jaxpr/id,jd->ij/dot_general | solution.py:19
  73.6 0.7 all_to_all.10
  74.3 4.6 %all-to-all-start.1 = ((f32[16,1,64]{2,1,0:T(1,128)}), f32[16,1,64]{2,1,0:T(1,128)S(1)}, u32[]{:S(2)}, u32[]{:S(2)}) async-start(f32[16,1,64]{2,1,0:T(1,128)} %all_to_all.10), calls=%async_computation.1 | async-start | bytes 16384 | tf_op jit(solution)/shard_map/all_to_all | solution.py:68
  79.0 6.4 %all-to-all-done.1 = f32[16,1,64]{2,1,0:T(1,128)S(1)} async-done(((f32[16,1,64]{2,1,0:T(1,128)}), f32[16,1,64]{2,1,0:T(1,128)S(1)}, u32[]{:S(2)}, u32[]{:S(2)}) %all-to-all-start.1) | async-done | bytes 4128 | tf_op jit(solution)/shard_map/all_to_all | solution.py:68
  85.4 0.5 broadcast.80
  85.9 0.7 reduce.4
  86.5 0.1 reshape.72
  86.6 3.2 %gather_fusion.1 = f32[768]{0:T(1024)S(1)} fusion(f32[1024]{0:T(1024)S(1)} %reshape.72, s32[1024]{0:T(1024)S(1)} %pad_clamp_fusion), kind=kCustom, calls=%fused_computation.1 | custom fusion | bytes 9216 | tf_op jit(solution)/shard_map/jit(_take)/gather | solution.py:71
  89.8 0.6 select_maximum_fusion
  (13 shorter events, 0.1 us)
Async XLA Ops:
  0.0 9.8 %copy-start = (f32[768,768]{1,0:T(8,128)S(1)}, f32[768,768]{1,0:T(8,128)}, u32[]{:S(2)}) copy-start(f32[768,768]{1,0:T(8,128)} %param.4) | copy-start | bytes 7077892
  57.7 3.8 %collective-permute-start = (bf16[1024,768]{1,0:T(8,128)(2,1)S(1)}, bf16[1024,768]{1,0:T(8,128)(2,1)S(1)}, u32[]{:S(2)}, u32[]{:S(2)}) collective-permute-start(bf16[1024,768]{1,0:T(8,128)(2,1)S(1)} %bitcast.25), channel_id=1, source_target_pairs={{0,1},{1,0},{2,3},{3,2},{4,5},{5,4},{6,7},{7,6},{8,9},{9,8},{10,11... | collective-permute-start | bytes 4718600 | tf_op jit(solution)/shard_map/ppermute | solution.py:15
  74.3 11.1 %all-to-all-start.1 = ((f32[16,1,64]{2,1,0:T(1,128)}), f32[16,1,64]{2,1,0:T(1,128)S(1)}, u32[]{:S(2)}, u32[]{:S(2)}) async-start(f32[16,1,64]{2,1,0:T(1,128)} %all_to_all.10), calls=%async_computation.1 | async-start | bytes 16384 | tf_op jit(solution)/shard_map/all_to_all | solution.py:68
where the time goes:
time: 90.8 us; the launch traced here: 90.4 us
  blocking collectives  43.3 us (48%)
  local copies, waits for them, and re-layouts  13.8 us (15%)
  other arithmetic  9.93 us (11%)
  waiting for transfers between devices  8.95 us (10%)
  starting transfers between devices  5.4 us (6%)
  matrix products  4.72 us (5%)
  loops' own time  4.19 us (5%)
    all_to_all x1, blocking collectives, on_device(): lax.all_to_all(outgoing, 'owners', split_axis=0, concat_axis=0, tiled=True)  43.3 us
    all_to_all x1, waiting for transfers between devices, on_device(): lax.all_to_all(best_slots.reshape(owners, capacity), 'owners', split_axis...  6.39 us
    dot_general x4, matrix products, scored(): jnp.einsum('id,jd->ij', queries, key_block, preferred_element_type=jnp.fl...  4.72 us
    all_to_all x1, starting transfers between devices, on_device(): lax.all_to_all(best_slots.reshape(owners, capacity), 'owners', split_axis...  4.63 us
    another operation x1, loops' own time, on_device(): best_slots = lax.map(both_tile, tile_starts).reshape(block_rows)  4.19 us
    gather x1, local copies, waits for them, and re-layouts, on_device(): jnp.take(padded, row_table, axis=0).reshape(owners, capacity, feature_width)  4 us
    scatter x1, local copies, waits for them, and re-layouts, on_device(): jnp.full((owners * capacity,), rows_dev, jnp.int32).at[slot_place]  3.38 us
    gather x1, local copies, waits for them, and re-layouts, on_device(): returned_best = jnp.take(answers.reshape(owners * capacity), slot_place)  3.18 us
  transfers between devices with their start and end apart: 2, of which 2 were waited for; matrix products, arithmetic and copies ran while one was open for 1% of the time, Pallas kernels for 0%

commit v1 on v0

v1 whole, which is shorter than its diff:
```python
import functools

import jax
import jax.numpy as jnp
from jax import lax
from jax.experimental import pallas as pl
from jax.experimental.pallas import tpu as pltpu
from jax.sharding import PartitionSpec as P

SLOTS = 1024
FLOOR = -4.0
DEAD = 4.0
VMEM_LIMIT = 40 * 2**20
LANES = 128


def block_mask(shape, lower, step):
    return lax.broadcasted_iota(jnp.int32, shape, 0) * step + lower


def row_slots(relative, clusters, capacity):
    rows = relative.shape[1]
    ids = lax.broadcasted_iota(jnp.int32, (clusters, LANES), 0)
    earlier = (
        lax.broadcasted_iota(jnp.int32, (LANES, LANES), 0)
        < lax.broadcasted_iota(jnp.int32, (LANES, LANES), 1)
    ).astype(jnp.bfloat16)
    carry = jnp.zeros((clusters, 1), jnp.float32)
    places = []
    for first in range(0, rows, LANES):
        part = relative[:, first : first + LANES]
        member = (ids == part).astype(jnp.float32)
        before = carry + jnp.dot(
            member.astype(jnp.bfloat16), earlier, preferred_element_type=jnp.float32
        )
        place = jnp.sum(before * member, axis=0, keepdims=True)
        places.append(part * capacity + place.astype(jnp.int32))
        carry = carry + jnp.sum(member, axis=1, keepdims=True)
    return jnp.concatenate(places, axis=1), carry


def pack_kernel(first_block, steps, clusters, capacity, relative_ref, rows_ref, *refs):
    *block_refs, slot_ref, unit_ref, pick_ref, count_ref = refs
    step = pl.program_id(0)
    tile = rows_ref.shape[0]
    values = rows_ref[...]
    scale = lax.rsqrt(jnp.sum(values * values, axis=1, keepdims=True) + 1e-06)
    unit_ref[pl.ds(pl.multiple_of(step * tile, tile), tile), :] = (values * scale).astype(jnp.bfloat16)

    @pl.when(step == 0)
    def _():
        slots, counts = row_slots(relative_ref[...], clusters, capacity)
        slot_ref[...] = slots
        count_ref[...] = jnp.broadcast_to(counts, count_ref.shape)
        wanted = lax.broadcasted_iota(jnp.int32, pick_ref.shape, 0) + first_block * capacity
        pick_ref[...] = (wanted == slots).astype(jnp.float32).astype(jnp.bfloat16)

    @pl.when(step == steps - 1)
    def _():
        lane = lax.broadcasted_iota(jnp.int32, (1, LANES), 1)
        done = 0
        for block_ref in block_refs:
            for start in range(0, block_ref.shape[0], capacity):
                size = capacity
                block = jnp.dot(
                    pick_ref[done : done + size, :], unit_ref[...], preferred_element_type=jnp.float32
                )
                which = first_block + done // capacity
                count = count_ref[which : which + 1, :]
                place = lax.broadcasted_iota(jnp.int32, (size, LANES), 0).astype(jnp.float32)
                mark = jnp.where((place >= count) & (lane == 0), DEAD, 0.0)
                block_ref[start : start + size, :LANES] = (block[:, :LANES] + mark).astype(jnp.bfloat16)
                block_ref[start : start + size, LANES:] = block[:, LANES:].astype(jnp.bfloat16)
                done += size


def pack(relative, embeddings, first_block, block_counts, clusters, capacity):
    rows, width = embeddings.shape
    steps = 3 if rows % 384 == 0 else 1
    total = sum(block_counts) * capacity
    whole = lambda shape: pl.BlockSpec(shape, lambda step: (0, 0))
    shapes = [(count * capacity, width) for count in block_counts]
    *blocks, slots = pl.pallas_call(
        functools.partial(pack_kernel, first_block, steps, clusters, capacity),
        grid=(steps,),
        in_specs=[whole((1, rows)), pl.BlockSpec((rows // steps, width), lambda step: (step, 0))],
        out_specs=[whole(shape) for shape in shapes] + [whole((1, rows))],
        out_shape=[jax.ShapeDtypeStruct(shape, jnp.bfloat16) for shape in shapes]
        + [jax.ShapeDtypeStruct((1, rows), jnp.int32)],
        scratch_shapes=[
            pltpu.VMEM((rows, width), jnp.bfloat16),
            pltpu.VMEM((total, rows), jnp.bfloat16),
            pltpu.VMEM((clusters, LANES), jnp.float32),
        ],
        compiler_params=pltpu.CompilerParams(vmem_limit_bytes=VMEM_LIMIT),
        cost_estimate=pl.CostEstimate(
            flops=2 * total * rows * width, bytes_accessed=rows * width * 4 + total * width * 2, transcendentals=rows
        ),
    )(relative, embeddings)
    return blocks, slots


def pieces(refs, tile):
    groups, current, held = [], [], 0
    for ref in refs:
        start = 0
        while start < ref.shape[0]:
            size = min(tile - held, ref.shape[0] - start)
            current.append((ref, start, size))
            start += size
            held += size
            if held == tile:
                groups.append(current)
                current, held = [], 0
    if current:
        groups.append(current)
    return groups


def load(group):
    parts = [ref[start : start + size, :] for ref, start, size in group]
    return parts[0] if len(parts) == 1 else jnp.concatenate(parts, axis=0)


def score_kernel(n_queries, n_keys, has_start, self_offset, *refs):
    query_refs = refs[:n_queries]
    key_refs = refs[n_queries : n_queries + n_keys]
    start_ref = refs[n_queries + n_keys] if has_start else None
    best_ref = refs[-1]
    key_groups = pieces(key_refs, 512)
    keys_and_bias = []
    query_first = 0
    for query_group in pieces(query_refs, 256):
        query = load(query_group)
        wide = query.shape[0]
        best = jnp.full((8, wide), FLOOR, jnp.float32)
        key_first = 0
        for key_group in key_groups:
            key = load(key_group)
            deep = key.shape[0]
            scores = lax.dot_general(key, query, (((1,), (1,)), ((), ())), preferred_element_type=jnp.float32)
            dead = key[:, :1].astype(jnp.float32) > 2.0
            drop = jnp.where(dead, 2 * FLOOR, 0.0)
            scores = scores + drop
            if self_offset is not None:
                shift = query_first + self_offset - key_first
                if -wide < shift < deep:
                    own = lax.broadcasted_iota(jnp.int32, scores.shape, 0) == (
                        lax.broadcasted_iota(jnp.int32, scores.shape, 1) + shift
                    )
                    scores = jnp.where(own, FLOOR, scores)
            best = jnp.maximum(best, jnp.max(scores.reshape(deep // 8, 8, wide), axis=0))
            key_first += deep
        row = jnp.max(best, axis=0, keepdims=True)
        for lane in range(0, wide, LANES):
            at = (query_first + lane) // LANES
            part = row[:, lane : lane + LANES]
            if start_ref is not None:
                part = jnp.maximum(part, start_ref[at : at + 1, :])
            best_ref[at : at + 1, :] = part
        query_first += wide


def score(queries, keys, self_offset, start=None):
    n_query = sum(block.shape[0] for block in queries)
    n_key = sum(block.shape[0] for block in keys)
    width = queries[0].shape[1]
    args = [*queries, *keys] + ([] if start is None else [start])
    return pl.pallas_call(
        functools.partial(score_kernel, len(queries), len(keys), start is not None, self_offset),
        in_specs=[pl.BlockSpec(memory_space=pltpu.VMEM)] * len(args),
        out_specs=pl.BlockSpec(memory_space=pltpu.VMEM),
        out_shape=jax.ShapeDtypeStruct((n_query // LANES, LANES), jnp.float32),
        compiler_params=pltpu.CompilerParams(vmem_limit_bytes=VMEM_LIMIT),
        cost_estimate=pl.CostEstimate(
            flops=2 * n_query * n_key * width, bytes_accessed=(n_query + n_key) * width * 2, transcendentals=0
        ),
    )(*args)


def lookup_kernel(capacity, slot_ref, answer_ref, out_ref):
    slots = slot_ref[...]
    clusters = answer_ref.shape[0]
    shift = capacity.bit_length() - 1
    place = lax.bitwise_and(slots, capacity - 1)
    which = lax.shift_right_logical(slots, shift)
    rows = slots.shape[1]
    pick = (lax.broadcasted_iota(jnp.int32, (capacity, rows), 0) == place).astype(jnp.float32).astype(jnp.bfloat16)
    rest = answer_ref[...]
    total = jnp.zeros((clusters, rows), jnp.float32)
    for _ in range(3):
        part = rest.astype(jnp.bfloat16)
        rest = rest - part.astype(jnp.float32)
        total = total + jnp.dot(part, pick, preferred_element_type=jnp.float32)
    mine = lax.broadcasted_iota(jnp.int32, (clusters, rows), 0) == which
    found = jnp.sum(jnp.where(mine, total, 0.0), axis=0, keepdims=True)
    out_ref[...] = jnp.maximum(found, -1.0)


def lookup(slots, answers, capacity):
    return pl.pallas_call(
        functools.partial(lookup_kernel, capacity),
        in_specs=[pl.BlockSpec(memory_space=pltpu.VMEM)] * 2,
        out_specs=pl.BlockSpec(memory_space=pltpu.VMEM),
        out_shape=jax.ShapeDtypeStruct(slots.shape, jnp.float32),
        compiler_params=pltpu.CompilerParams(vmem_limit_bytes=VMEM_LIMIT),
    )(slots, answers)


def by_xor(value, axis, mask):
    return lax.ppermute(value, axis, [(source, source ^ mask) for source in range(lax.axis_size(axis))])


def on_device(embeddings, cluster_of):
    owners = lax.axis_size("owners")
    clusters = owners // 2
    capacity = SLOTS // clusters
    rows = embeddings.shape[0]
    cluster_row = cluster_of.reshape(1, rows)
    chip = lax.axis_index("owners") // 2
    same_core = [list(range(core, owners, 2)) for core in range(2)]
    if clusters == 8:
        relative = cluster_row ^ chip
        far_out, slots = pack(relative, embeddings, 4, [1, 1, 1, 1], clusters, capacity)
        far = [by_xor(block, "owners", 2 * mask) for block, mask in zip(far_out, (4, 5, 6, 7))]
        near_out, _ = pack(relative, embeddings, 0, [1, 1, 1, 1], clusters, capacity)
        near = [near_out[0]] + [by_xor(block, "owners", 2 * mask) for block, mask in zip(near_out[1:], (1, 2, 3))]
        near_other = [by_xor(block, "owners", 1) for block in near]
        near_best = score(near, near + near_other, 0)
        far_other = [by_xor(block, "owners", 1) for block in far]
        near_best = score(near, far + far_other, None, near_best)
        far_best = score(far, far + near + near_other + far_other, 0)
        best = jnp.concatenate([near_best, far_best], axis=0)
        order = jnp.arange(clusters, dtype=jnp.int32) ^ chip
        best = jnp.take(best, order, axis=0)
        answers = lax.all_to_all(best, "owners", 0, 0, axis_index_groups=same_core, tiled=True)
        answers = jnp.take(answers, order, axis=0)
    else:
        (outgoing,), slots = pack(cluster_row, embeddings, 0, [clusters], clusters, capacity)
        own = lax.all_to_all(
            outgoing.reshape(clusters, capacity, -1), "owners", 0, 0, axis_index_groups=same_core, tiled=True
        ).reshape(SLOTS, -1)
        best = score([own], [own, by_xor(own, "owners", 1)], 0).reshape(clusters, capacity)
        answers = lax.all_to_all(best, "owners", 0, 0, axis_index_groups=same_core, tiled=True)
    return lookup(slots, answers, capacity).reshape(rows)


def solution(mesh):
    placed = (P(("groups", "owners"), None), P(("groups", "owners")))
    return jax.shard_map(
        on_device, mesh=mesh, in_specs=placed, out_specs=P(("groups", "owners")), check_vma=False
    )
```

time: 90.8 us -> 61.1 us (0.67)
  blocking collectives: 43.3 us -> 11.2 us
  waiting for transfers between devices: 8.95 us -> 22.9 us
  local copies, waits for them, and re-layouts: 13.8 us -> 2.78 us
  starting transfers between devices: 5.4 us -> 14.5 us
  other arithmetic: 9.93 us -> 1.47 us
  Pallas kernels: 0 us -> 8 us
  matrix products: 4.72 us -> 0 us
  loops' own time: 4.19 us -> 0 us
    all_to_all x1, blocking collectives: 43.3 us -> 11.2 us  [on_device(): lax.all_to_all(best, 'owners', 0, 0, axis_index_groups=same_core, tiled=T...]
    ppermute x1 -> x15, waiting for transfers between devices: 2.56 us -> 22.9 us  [by_xor(): lax.ppermute(value, axis, [(source, source ^ mask) for source in range(la...]
    ppermute x1 -> x15, starting transfers between devices: 0.77 us -> 14.5 us  [by_xor(): lax.ppermute(value, axis, [(source, source ^ mask) for source in range(la...]
    pallas_call x0 -> x6, Pallas kernels: none -> 8 us  [the longest x3 3.91 us: score(): pl.pallas_call(functools.partial(score_kernel, len(queries), len(keys), s...]
    all_to_all x1 -> x0, waiting for transfers between devices: 6.39 us -> none  [on_device(): lax.all_to_all(best_slots.reshape(owners, capacity), 'owners', split_axis...]
    gather x2, local copies, waits for them, and re-layouts: 7.19 us -> 1.11 us  [the longest x1 0.56 us: on_device(): best = jnp.take(best, order, axis=0)]
    dot_general x4 -> x0, matrix products: 4.72 us -> none  [scored(): jnp.einsum('id,jd->ij', queries, key_block, preferred_element_type=jnp.fl...]
    all_to_all x1 -> x0, starting transfers between devices: 4.63 us -> none  [on_device(): lax.all_to_all(best_slots.reshape(owners, capacity), 'owners', split_axis...]
  transfers between devices with their start and end apart: 2 -> 15, of which waited for: 2 -> 5; matrix products, arithmetic and copies ran while one was open for 1% -> 0% of each run, Pallas kernels for 0% -> 5%
where the time goes in v1:
time: 61.1 us; the launch traced here: 60.9 us
  waiting for transfers between devices  22.9 us (37%)
  starting transfers between devices  14.5 us (24%)
  blocking collectives  11.2 us (18%)
  Pallas kernels  8 us (13%)
  local copies, waits for them, and re-layouts  2.78 us (5%)
  other arithmetic  1.47 us (2%)
    ppermute x15, waiting for transfers between devices, by_xor(): lax.ppermute(value, axis, [(source, source ^ mask) for source in range(la...  22.9 us
    ppermute x15, starting transfers between devices, by_xor(): lax.ppermute(value, axis, [(source, source ^ mask) for source in range(la...  14.5 us
    all_to_all x1, blocking collectives, on_device(): lax.all_to_all(best, 'owners', 0, 0, axis_index_groups=same_core, tiled=T...  11.2 us
    pallas_call x3, Pallas kernels, score(): pl.pallas_call(functools.partial(score_kernel, len(queries), len(keys), s...  3.91 us
    pallas_call x2, Pallas kernels, pack(): pl.pallas_call(functools.partial(pack_kernel, first_block, steps, cluster...  3.87 us
    unnamed x2, local copies, waits for them, and re-layouts  1.66 us
  transfers between devices with their start and end apart: 15, of which 5 were waited for; matrix products, arithmetic and copies ran while one was open for 0% of the time, Pallas kernels for 5%

profile of v1, /device:TPU:0, one launch (start us, length us, event | category | flops | bytes accessed | tf_op | source)
XLA Modules:
  0.0 60.9 jit_solution(18074955113664157338)
XLA Ops:
  0.0 0.7 %broadcast_xor_fusion = s32[768]{0:T(1024)S(1)} fusion(s32[768]{0:T(1024)} %param.5, s32[]{:T(128)S(6)} %select_n.12), kind=kLoop, calls=%fused_computation.7 | loop fusion | flops 768 | bytes 6148 | tf_op jit(solution)/shard_map/xor | solution.py:223
  0.7 0.0 copy-start
  0.7 1.7 %copy-done = f32[768,768]{1,0:T(8,128)S(1)} copy-done((f32[768,768]{1,0:T(8,128)S(1)}, f32[768,768]{1,0:T(8,128)}, u32[]{:S(2)}) %copy-start) | copy-done | bytes 2359320
  2.4 1.6 %shard_map.28 = (bf16[128,768]{1,0:T(8,128)(2,1)S(1)}, bf16[128,768]{1,0:T(8,128)(2,1)S(1)}, bf16[128,768]{1,0:T(8,128)(2,1)S(1)}, bf16[128,768]{1,0:T(8,128)(2,1)S(1)}, s32[1,768]{1,0:T(1,128)S(1)}) custom-call(s32[1,768]{1,0:T(1,128)S(1)} %xor.16.relative_ref, f32[768,768]{1,0:T(8,128)S(1)} %copy-done), custom_call_target="tpu_custom_call" | custom-call | flops 603979776 | bytes 3145728 | tf_op jit(solution)/shard_map/pallas_call | solution.py:83
  4.0 4.1 %collective-permute-start.3 = (bf16[128,768]{1,0:T(8,128)(2,1)S(1)}, bf16[128,768]{1,0:T(8,128)(2,1)S(1)}, u32[]{:S(2)}, u32[]{:S(2)}) collective-permute-start(bf16[128,768]{1,0:T(8,128)(2,1)S(1)} %get-tuple-element.20), channel_id=1, source_target_pairs={{0,8},{1,9},{2,10},{3,11},{4,12},{5,13},{6,14},{7,15},{8,0},{9,1},... | collective-permute-start | bytes 589832 | tf_op jit(solution)/shard_map/ppermute | solution.py:211
  8.1 1.3 %collective-permute-start.4 = (bf16[128,768]{1,0:T(8,128)(2,1)S(1)}, bf16[128,768]{1,0:T(8,128)(2,1)S(1)}, u32[]{:S(2)}, u32[]{:S(2)}) collective-permute-start(bf16[128,768]{1,0:T(8,128)(2,1)S(1)} %get-tuple-element.21), channel_id=1, source_target_pairs={{0,10},{1,11},{2,8},{3,9},{4,14},{5,15},{6,12},{7,13},{8,2},{9,3},... | collective-permute-start | bytes 589832 | tf_op jit(solution)/shard_map/ppermute | solution.py:211
  9.4 3.6 %collective-permute-start.5 = (bf16[128,768]{1,0:T(8,128)(2,1)S(1)}, bf16[128,768]{1,0:T(8,128)(2,1)S(1)}, u32[]{:S(2)}, u32[]{:S(2)}) collective-permute-start(bf16[128,768]{1,0:T(8,128)(2,1)S(1)} %get-tuple-element.22), channel_id=1, source_target_pairs={{0,12},{1,13},{2,14},{3,15},{4,8},{5,9},{6,10},{7,11},{8,4},{9,5},... | collective-permute-start | bytes 589832 | tf_op jit(solution)/shard_map/ppermute | solution.py:211
  13.0 2.3 %shard_map.29 = (bf16[128,768]{1,0:T(8,128)(2,1)S(1)}, bf16[128,768]{1,0:T(8,128)(2,1)S(1)}, bf16[128,768]{1,0:T(8,128)(2,1)S(1)}, bf16[128,768]{1,0:T(8,128)(2,1)S(1)}, s32[1,768]{1,0:T(1,128)}) custom-call(s32[1,768]{1,0:T(1,128)S(1)} %xor.16.relative_ref, f32[768,768]{1,0:T(8,128)S(1)} %copy-done), custom_call_target="tpu_custom_call" | custom-call | flops 603979776 | bytes 3145728 | tf_op jit(solution)/shard_map/pallas_call | solution.py:83
  15.2 0.5 collective-permute-start
  15.7 0.0 collective-permute-start.1
  15.8 10.8 %collective-permute-done.3.refs_4_.refs_0_ = bf16[128,768]{1,0:T(8,128)(2,1)S(1)} collective-permute-done((bf16[128,768]{1,0:T(8,128)(2,1)S(1)}, bf16[128,768]{1,0:T(8,128)(2,1)S(1)}, u32[]{:S(2)}, u32[]{:S(2)}) %collective-permute-start.3) | collective-permute-done | bytes 196640 | tf_op jit(solution)/shard_map/ppermute | solution.py:211
  26.5 0.9 %collective-permute-start.2 = (bf16[128,768]{1,0:T(8,128)(2,1)S(1)}, bf16[128,768]{1,0:T(8,128)(2,1)S(1)}, u32[]{:S(2)}, u32[]{:S(2)}) collective-permute-start(bf16[128,768]{1,0:T(8,128)(2,1)S(1)} %get-tuple-element.19), channel_id=1, source_target_pairs={{0,6},{1,7},{2,4},{3,5},{4,2},{5,3},{6,0},{7,1},{8,14},{9,15},{10,... | collective-permute-start | bytes 589832 | tf_op jit(solution)/shard_map/ppermute | solution.py:211
  27.4 4.6 %collective-permute-done.4.refs_5_.refs_1_ = bf16[128,768]{1,0:T(8,128)(2,1)S(1)} collective-permute-done((bf16[128,768]{1,0:T(8,128)(2,1)S(1)}, bf16[128,768]{1,0:T(8,128)(2,1)S(1)}, u32[]{:S(2)}, u32[]{:S(2)}) %collective-permute-start.4) | collective-permute-done | bytes 196640 | tf_op jit(solution)/shard_map/ppermute | solution.py:211
  32.0 2.4 %collective-permute-start.6 = (bf16[128,768]{1,0:T(8,128)(2,1)S(1)}, bf16[128,768]{1,0:T(8,128)(2,1)S(1)}, u32[]{:S(2)}, u32[]{:S(2)}) collective-permute-start(bf16[128,768]{1,0:T(8,128)(2,1)S(1)} %get-tuple-element.23), channel_id=1, source_target_pairs={{0,14},{1,15},{2,12},{3,13},{4,10},{5,11},{6,8},{7,9},{8,6},{9,7},... | collective-permute-start | bytes 589832 | tf_op jit(solution)/shard_map/ppermute | solution.py:211
  34.4 0.0 collective-permute-done.5.refs_6_.refs_2_
  34.4 0.0 collective-permute-start.11
  34.4 0.0 collective-permute-done.refs_1_.refs_5_.refs_9_
  34.4 0.5 collective-permute-start.12
  34.9 0.0 collective-permute-done.1.refs_2_.refs_6_.refs_10_
  34.9 0.1 collective-permute-start.13
  35.0 7.1 %collective-permute-done.2.refs_3_.refs_7_.refs_11_ = bf16[128,768]{1,0:T(8,128)(2,1)S(1)} collective-permute-done((bf16[128,768]{1,0:T(8,128)(2,1)S(1)}, bf16[128,768]{1,0:T(8,128)(2,1)S(1)}, u32[]{:S(2)}, u32[]{:S(2)}) %collective-permute-start.2) | collective-permute-done | bytes 196640 | tf_op jit(solution)/shard_map/ppermute | solution.py:211
  42.1 0.0 collective-permute-start.14
  42.1 0.0 collective-permute-done.6.refs_7_.refs_3_
  42.1 0.5 collective-permute-start.7
  42.6 0.0 collective-permute-done.11.refs_8_.refs_12_
  42.7 0.1 collective-permute-start.8
  42.7 0.0 collective-permute-done.12.refs_9_.refs_13_
  42.7 0.4 collective-permute-start.9
  43.2 0.0 collective-permute-done.13.refs_10_.refs_14_
  43.2 0.1 collective-permute-start.10
  43.3 0.3 collective-permute-done.14.refs_11_.refs_15_
  43.6 1.0 %shard_map.30.refs_12_ = f32[4,128]{1,0:T(4,128)S(1)} custom-call(bf16[128,768]{1,0:T(8,128)(2,1)S(1)} %get-tuple-element.16.refs_0_.refs_4_.refs_8_, bf16[128,768]{1,0:T(8,128)(2,1)S(1)} %collective-permute-done.refs_1_.refs_5_.refs_9_, bf16[128,768]{1,0:T(8,128)(2,1)S(1)} %collective-permute-done.1.refs_2_.refs_6_.refs_10_, ...), custom_call_target="tpu_custom_call" | custom-call | flops 805306368 | bytes 2359296 | tf_op jit(solution)/shard_map/pallas_call | solution.py:169
  44.6 0.0 collective-permute-done.7.refs_8_.refs_16_
  44.6 0.0 collective-permute-done.8.refs_9_.refs_17_
  44.6 0.0 collective-permute-done.9.refs_10_.refs_18_
  44.6 0.1 collective-permute-done.10.refs_11_.refs_19_
  44.7 1.9 %shard_map.32 = f32[4,128]{1,0:T(4,128)S(1)} custom-call(bf16[128,768]{1,0:T(8,128)(2,1)S(1)} %collective-permute-done.3.refs_4_.refs_0_, bf16[128,768]{1,0:T(8,128)(2,1)S(1)} %collective-permute-done.4.refs_5_.refs_1_, bf16[128,768]{1,0:T(8,128)(2,1)S(1)} %collective-permute-done.5.refs_6_.refs_2_, ...), custom_call_target="tpu_custom_call" | custom-call | flops 1610612736 | bytes 3932160 | tf_op jit(solution)/shard_map/pallas_call | solution.py:169
  46.6 1.0 %shard_map.31 = f32[4,128]{1,0:T(4,128)S(1)} custom-call(bf16[128,768]{1,0:T(8,128)(2,1)S(1)} %get-tuple-element.16.refs_0_.refs_4_.refs_8_, bf16[128,768]{1,0:T(8,128)(2,1)S(1)} %collective-permute-done.refs_1_.refs_5_.refs_9_, bf16[128,768]{1,0:T(8,128)(2,1)S(1)} %collective-permute-done.1.refs_2_.refs_6_.refs_10_, ...), custom_call_target="tpu_custom_call" | custom-call | flops 805306368 | bytes 2359296 | tf_op jit(solution)/shard_map/pallas_call | solution.py:169
  47.6 0.6 gather_fusion
  48.2 0.1 broadcast_select_fusion.1
  48.3 11.2 %all_to_all.12 = f32[8,1,128]{2,1,0:T(1,128)S(1)} all-to-all(f32[8,1,128]{2,1,0:T(1,128)S(1)} %bitcast.5), channel_id=1, replica_groups={{0,2,4,6,8,10,12,14},{1,3,5,7,9,11,13,15},{16,18,20,22,24,26,28,30},{17..., dimensions={0} | all-to-all | bytes 8192 | tf_op jit(solution)/shard_map/all_to_all | solution.py:236
  59.5 0.6 gather_fusion.1
  60.0 0.1 broadcast_select_fusion.answer_ref
  60.1 0.2 shard_map.33
  60.3 0.6 reduce
  (5 shorter events, 0.0 us)
Async XLA Ops:
  0.7 1.7 %copy-start = (f32[768,768]{1,0:T(8,128)S(1)}, f32[768,768]{1,0:T(8,128)}, u32[]{:S(2)}) copy-start(f32[768,768]{1,0:T(8,128)} %rows_ref.3) | copy-start | bytes 7077892
  4.0 22.6 %collective-permute-start.3 = (bf16[128,768]{1,0:T(8,128)(2,1)S(1)}, bf16[128,768]{1,0:T(8,128)(2,1)S(1)}, u32[]{:S(2)}, u32[]{:S(2)}) collective-permute-start(bf16[128,768]{1,0:T(8,128)(2,1)S(1)} %get-tuple-element.20), channel_id=1, source_target_pairs={{0,8},{1,9},{2,10},{3,11},{4,12},{5,13},{6,14},{7,15},{8,0},{9,1},... | collective-permute-start | bytes 589832 | tf_op jit(solution)/shard_map/ppermute | solution.py:211
  8.1 23.9 %collective-permute-start.4 = (bf16[128,768]{1,0:T(8,128)(2,1)S(1)}, bf16[128,768]{1,0:T(8,128)(2,1)S(1)}, u32[]{:S(2)}, u32[]{:S(2)}) collective-permute-start(bf16[128,768]{1,0:T(8,128)(2,1)S(1)} %get-tuple-element.21), channel_id=1, source_target_pairs={{0,10},{1,11},{2,8},{3,9},{4,14},{5,15},{6,12},{7,13},{8,2},{9,3},... | collective-permute-start | bytes 589832 | tf_op jit(solution)/shard_map/ppermute | solution.py:211
  9.4 25.0 %collective-permute-start.5 = (bf16[128,768]{1,0:T(8,128)(2,1)S(1)}, bf16[128,768]{1,0:T(8,128)(2,1)S(1)}, u32[]{:S(2)}, u32[]{:S(2)}) collective-permute-start(bf16[128,768]{1,0:T(8,128)(2,1)S(1)} %get-tuple-element.22), channel_id=1, source_target_pairs={{0,12},{1,13},{2,14},{3,15},{4,8},{5,9},{6,10},{7,11},{8,4},{9,5},... | collective-permute-start | bytes 589832 | tf_op jit(solution)/shard_map/ppermute | solution.py:211
  15.2 19.2 %collective-permute-start = (bf16[128,768]{1,0:T(8,128)(2,1)S(1)}, bf16[128,768]{1,0:T(8,128)(2,1)S(1)}, u32[]{:S(2)}, u32[]{:S(2)}) collective-permute-start(bf16[128,768]{1,0:T(8,128)(2,1)S(1)} %get-tuple-element.17), channel_id=1, source_target_pairs={{0,2},{1,3},{2,0},{3,1},{4,6},{5,7},{6,4},{7,5},{8,10},{9,11},{10,... | collective-permute-start | bytes 589832 | tf_op jit(solution)/shard_map/ppermute | solution.py:211
  15.7 19.2 %collective-permute-start.1 = (bf16[128,768]{1,0:T(8,128)(2,1)S(1)}, bf16[128,768]{1,0:T(8,128)(2,1)S(1)}, u32[]{:S(2)}, u32[]{:S(2)}) collective-permute-start(bf16[128,768]{1,0:T(8,128)(2,1)S(1)} %get-tuple-element.18), channel_id=1, source_target_pairs={{0,4},{1,5},{2,6},{3,7},{4,0},{5,1},{6,2},{7,3},{8,12},{9,13},{10,... | collective-permute-start | bytes 589832 | tf_op jit(solution)/shard_map/ppermute | solution.py:211
  26.5 15.6 %collective-permute-start.2 = (bf16[128,768]{1,0:T(8,128)(2,1)S(1)}, bf16[128,768]{1,0:T(8,128)(2,1)S(1)}, u32[]{:S(2)}, u32[]{:S(2)}) collective-permute-start(bf16[128,768]{1,0:T(8,128)(2,1)S(1)} %get-tuple-element.19), channel_id=1, source_target_pairs={{0,6},{1,7},{2,4},{3,5},{4,2},{5,3},{6,0},{7,1},{8,14},{9,15},{10,... | collective-permute-start | bytes 589832 | tf_op jit(solution)/shard_map/ppermute | solution.py:211
  32.0 10.1 %collective-permute-start.6 = (bf16[128,768]{1,0:T(8,128)(2,1)S(1)}, bf16[128,768]{1,0:T(8,128)(2,1)S(1)}, u32[]{:S(2)}, u32[]{:S(2)}) collective-permute-start(bf16[128,768]{1,0:T(8,128)(2,1)S(1)} %get-tuple-element.23), channel_id=1, source_target_pairs={{0,14},{1,15},{2,12},{3,13},{4,10},{5,11},{6,8},{7,9},{8,6},{9,7},... | collective-permute-start | bytes 589832 | tf_op jit(solution)/shard_map/ppermute | solution.py:211
  34.4 8.3 %collective-permute-start.11 = (bf16[128,768]{1,0:T(8,128)(2,1)S(1)}, bf16[128,768]{1,0:T(8,128)(2,1)S(1)}, u32[]{:S(2)}, u32[]{:S(2)}) collective-permute-start(bf16[128,768]{1,0:T(8,128)(2,1)S(1)} %get-tuple-element.16.refs_0_.refs_4_.refs_8_), channel_id=1, source_target_pairs={{0,1},{1,0},{2,3},{3,2},{4,5},{5,4},{6,7},{7,6},{8,9},{9,8},{10,11... | collective-permute-start | bytes 589832 | tf_op jit(solution)/shard_map/ppermute | solution.py:211
  34.4 8.3 %collective-permute-start.12 = (bf16[128,768]{1,0:T(8,128)(2,1)S(1)}, bf16[128,768]{1,0:T(8,128)(2,1)S(1)}, u32[]{:S(2)}, u32[]{:S(2)}) collective-permute-start(bf16[128,768]{1,0:T(8,128)(2,1)S(1)} %collective-permute-done.refs_1_.refs_5_.refs_9_), channel_id=1, source_target_pairs={{0,1},{1,0},{2,3},{3,2},{4,5},{5,4},{6,7},{7,6},{8,9},{9,8},{10,11... | collective-permute-start | bytes 589832 | tf_op jit(solution)/shard_map/ppermute | solution.py:211
  34.9 8.3 %collective-permute-start.13 = (bf16[128,768]{1,0:T(8,128)(2,1)S(1)}, bf16[128,768]{1,0:T(8,128)(2,1)S(1)}, u32[]{:S(2)}, u32[]{:S(2)}) collective-permute-start(bf16[128,768]{1,0:T(8,128)(2,1)S(1)} %collective-permute-done.1.refs_2_.refs_6_.refs_10_), channel_id=1, source_target_pairs={{0,1},{1,0},{2,3},{3,2},{4,5},{5,4},{6,7},{7,6},{8,9},{9,8},{10,11... | collective-permute-start | bytes 589832 | tf_op jit(solution)/shard_map/ppermute | solution.py:211
  42.1 1.4 %collective-permute-start.14 = (bf16[128,768]{1,0:T(8,128)(2,1)S(1)}, bf16[128,768]{1,0:T(8,128)(2,1)S(1)}, u32[]{:S(2)}, u32[]{:S(2)}) collective-permute-start(bf16[128,768]{1,0:T(8,128)(2,1)S(1)} %collective-permute-done.2.refs_3_.refs_7_.refs_11_), channel_id=1, source_target_pairs={{0,1},{1,0},{2,3},{3,2},{4,5},{5,4},{6,7},{7,6},{8,9},{9,8},{10,11... | collective-permute-start | bytes 589832 | tf_op jit(solution)/shard_map/ppermute | solution.py:211
  42.1 2.5 %collective-permute-start.7 = (bf16[128,768]{1,0:T(8,128)(2,1)S(1)}, bf16[128,768]{1,0:T(8,128)(2,1)S(1)}, u32[]{:S(2)}, u32[]{:S(2)}) collective-permute-start(bf16[128,768]{1,0:T(8,128)(2,1)S(1)} %collective-permute-done.3.refs_4_.refs_0_), channel_id=1, source_target_pairs={{0,1},{1,0},{2,3},{3,2},{4,5},{5,4},{6,7},{7,6},{8,9},{9,8},{10,11... | collective-permute-start | bytes 589832 | tf_op jit(solution)/shard_map/ppermute | solution.py:211
  42.7 2.0 %collective-permute-start.8 = (bf16[128,768]{1,0:T(8,128)(2,1)S(1)}, bf16[128,768]{1,0:T(8,128)(2,1)S(1)}, u32[]{:S(2)}, u32[]{:S(2)}) collective-permute-start(bf16[128,768]{1,0:T(8,128)(2,1)S(1)} %collective-permute-done.4.refs_5_.refs_1_), channel_id=1, source_target_pairs={{0,1},{1,0},{2,3},{3,2},{4,5},{5,4},{6,7},{7,6},{8,9},{9,8},{10,11... | collective-permute-start | bytes 589832 | tf_op jit(solution)/shard_map/ppermute | solution.py:211
  42.7 1.9 %collective-permute-start.9 = (bf16[128,768]{1,0:T(8,128)(2,1)S(1)}, bf16[128,768]{1,0:T(8,128)(2,1)S(1)}, u32[]{:S(2)}, u32[]{:S(2)}) collective-permute-start(bf16[128,768]{1,0:T(8,128)(2,1)S(1)} %collective-permute-done.5.refs_6_.refs_2_), channel_id=1, source_target_pairs={{0,1},{1,0},{2,3},{3,2},{4,5},{5,4},{6,7},{7,6},{8,9},{9,8},{10,11... | collective-permute-start | bytes 589832 | tf_op jit(solution)/shard_map/ppermute | solution.py:211
  43.2 1.5 %collective-permute-start.10 = (bf16[128,768]{1,0:T(8,128)(2,1)S(1)}, bf16[128,768]{1,0:T(8,128)(2,1)S(1)}, u32[]{:S(2)}, u32[]{:S(2)}) collective-permute-start(bf16[128,768]{1,0:T(8,128)(2,1)S(1)} %collective-permute-done.6.refs_7_.refs_3_), channel_id=1, source_target_pairs={{0,1},{1,0},{2,3},{3,2},{4,5},{5,4},{6,7},{7,6},{8,9},{9,8},{10,11... | collective-permute-start | bytes 589832 | tf_op jit(solution)/shard_map/ppermute | solution.py:211

commit v2 on v1

v2 whole, which is shorter than its diff:
```python
import functools

import jax
import jax.numpy as jnp
from jax import lax
from jax.experimental import pallas as pl
from jax.experimental.pallas import tpu as pltpu
from jax.sharding import PartitionSpec as P

SLOTS = 1024
FLOOR = -4.0
DEAD = 4.0
VMEM_LIMIT = 40 * 2**20
LANES = 128


def row_slots(relative, clusters, capacity):
    rows = relative.shape[1]
    ids = lax.broadcasted_iota(jnp.int32, (clusters, LANES), 0)
    earlier = (
        lax.broadcasted_iota(jnp.int32, (LANES, LANES), 0)
        < lax.broadcasted_iota(jnp.int32, (LANES, LANES), 1)
    ).astype(jnp.bfloat16)
    carry = jnp.zeros((clusters, 1), jnp.float32)
    places = []
    for first in range(0, rows, LANES):
        part = relative[:, first : first + LANES]
        member = (ids == part).astype(jnp.float32)
        before = carry + jnp.dot(
            member.astype(jnp.bfloat16), earlier, preferred_element_type=jnp.float32
        )
        place = jnp.sum(before * member, axis=0, keepdims=True)
        places.append(part * capacity + place.astype(jnp.int32))
        carry = carry + jnp.sum(member, axis=1, keepdims=True)
    return jnp.concatenate(places, axis=1), carry


def pack_kernel(first_block, mixed, clusters, capacity, cluster_ref, rows_ref, *refs):
    *block_refs, slot_ref, held_ref, unit_ref, pick_ref, sems = refs
    steps, tile, _ = held_ref.shape
    copies = [
        pltpu.make_async_copy(rows_ref.at[pl.ds(step * tile, tile), :], held_ref.at[step], sems.at[step])
        for step in range(steps)
    ]
    for copy in copies:
        copy.start()
    relative = cluster_ref[...]
    if mixed:
        relative = lax.bitwise_xor(relative, lax.axis_index("owners") // 2)
    slots, counts = row_slots(relative, clusters, capacity)
    slot_ref[...] = slots
    wanted = lax.broadcasted_iota(jnp.int32, pick_ref.shape, 0) + first_block * capacity
    pick_ref[...] = (wanted == slots).astype(jnp.float32).astype(jnp.bfloat16)
    for step, copy in enumerate(copies):
        copy.wait()
        values = held_ref[step]
        scale = lax.rsqrt(jnp.sum(values * values, axis=1, keepdims=True) + 1e-06)
        unit_ref[step * tile : (step + 1) * tile, :] = (values * scale).astype(jnp.bfloat16)
    lane = lax.broadcasted_iota(jnp.int32, (capacity, LANES), 1)
    place = lax.broadcasted_iota(jnp.int32, (capacity, LANES), 0).astype(jnp.float32)
    done = 0
    for block_ref in block_refs:
        for start in range(0, block_ref.shape[0], capacity):
            block = jnp.dot(
                pick_ref[done : done + capacity, :], unit_ref[...], preferred_element_type=jnp.float32
            )
            which = first_block + done // capacity
            mark = jnp.where((place >= counts[which : which + 1, :]) & (lane == 0), DEAD, 0.0)
            block_ref[start : start + capacity, :LANES] = (block[:, :LANES] + mark).astype(jnp.bfloat16)
            block_ref[start : start + capacity, LANES:] = block[:, LANES:].astype(jnp.bfloat16)
            done += capacity


def pack(cluster_row, embeddings, first_block, block_counts, clusters, capacity, mixed):
    rows, width = embeddings.shape
    steps = 3 if rows % 384 == 0 else 1
    total = sum(block_counts) * capacity
    vmem = pl.BlockSpec(memory_space=pltpu.VMEM)
    *blocks, slots = pl.pallas_call(
        functools.partial(pack_kernel, first_block, mixed, clusters, capacity),
        in_specs=[vmem, pl.BlockSpec(memory_space=pltpu.HBM)],
        out_specs=[vmem] * (len(block_counts) + 1),
        out_shape=[jax.ShapeDtypeStruct((count * capacity, width), jnp.bfloat16) for count in block_counts]
        + [jax.ShapeDtypeStruct((1, rows), jnp.int32)],
        scratch_shapes=[
            pltpu.VMEM((steps, rows // steps, width), jnp.float32),
            pltpu.VMEM((rows, width), jnp.bfloat16),
            pltpu.VMEM((total, rows), jnp.bfloat16),
            pltpu.SemaphoreType.DMA((steps,)),
        ],
        compiler_params=pltpu.CompilerParams(vmem_limit_bytes=VMEM_LIMIT),
        cost_estimate=pl.CostEstimate(
            flops=2 * total * rows * width, bytes_accessed=rows * width * 4 + total * width * 2, transcendentals=rows
        ),
    )(cluster_row, embeddings)
    return blocks, slots


def pieces(refs, tile):
    groups, current, held = [], [], 0
    for ref in refs:
        start = 0
        while start < ref.shape[0]:
            size = min(tile - held, ref.shape[0] - start)
            current.append((ref, start, size))
            start += size
            held += size
            if held == tile:
                groups.append(current)
                current, held = [], 0
    if current:
        groups.append(current)
    return groups


def load(group):
    parts = [ref[start : start + size, :] for ref, start, size in group]
    return parts[0] if len(parts) == 1 else jnp.concatenate(parts, axis=0)


def tile_best(key, query, shift):
    deep, wide = key.shape[0], query.shape[0]
    scores = lax.dot_general(key, query, (((1,), (1,)), ((), ())), preferred_element_type=jnp.float32)
    dead = key[:, :1].astype(jnp.float32) > 2.0
    scores = scores + jnp.where(dead, 2 * FLOOR, 0.0)
    if shift is not None and -wide < shift < deep:
        own = lax.broadcasted_iota(jnp.int32, scores.shape, 0) == (
            lax.broadcasted_iota(jnp.int32, scores.shape, 1) + shift
        )
        scores = jnp.where(own, FLOOR, scores)
    return jnp.max(scores.reshape(deep // 8, 8, wide), axis=0)


def score_kernel(n_own, n_other, n_old, mixed, *refs):
    own_refs = refs[:n_own]
    other_refs = refs[n_own : n_own + n_other]
    start_ref = refs[n_own + n_other] if n_old else None
    best_ref = refs[-1]
    per_ref = own_refs[0].shape[0] // LANES
    chip = lax.axis_index("owners") // 2 if mixed else 0

    def run(query_refs, query_first, key_sets, has_start):
        at = query_first
        for query_group in pieces(query_refs, 256):
            query = load(query_group)
            wide = query.shape[0]
            best = jnp.full((8, wide), FLOOR, jnp.float32)
            for key_refs, key_first in key_sets:
                for key_group in pieces(key_refs, 512):
                    key = load(key_group)
                    best = jnp.maximum(best, tile_best(key, query, None if key_first is None else at - key_first))
                    if key_first is not None:
                        key_first += key.shape[0]
            row = jnp.max(best, axis=0, keepdims=True)
            for lane in range(0, wide, LANES):
                index = (at + lane) // LANES
                part = row[:, lane : lane + LANES]
                if has_start:
                    part = jnp.maximum(part, start_ref[index : index + 1, :])
                best_ref[pl.ds(lax.bitwise_xor(index, chip) if mixed else index, 1), :] = part
            at += wide

    old = n_old * per_ref * LANES
    if n_old:
        run(own_refs[:n_old], 0, [(own_refs[n_old:], old), (other_refs[n_old:], None)], True)
    run(own_refs[n_old:], old, [(own_refs, 0), (other_refs, None)], False)


def score(own, other, n_old=0, start=None, mixed=False):
    n_own = sum(block.shape[0] for block in own)
    n_key = n_own + sum(block.shape[0] for block in other)
    width = own[0].shape[1]
    args = [*own, *other] + ([] if start is None else [start])
    return pl.pallas_call(
        functools.partial(score_kernel, len(own), len(other), n_old, mixed),
        in_specs=[pl.BlockSpec(memory_space=pltpu.VMEM)] * len(args),
        out_specs=pl.BlockSpec(memory_space=pltpu.VMEM),
        out_shape=jax.ShapeDtypeStruct((n_own // LANES, LANES), jnp.float32),
        compiler_params=pltpu.CompilerParams(vmem_limit_bytes=VMEM_LIMIT),
        cost_estimate=pl.CostEstimate(
            flops=2 * n_own * n_key * width, bytes_accessed=n_key * width * 2, transcendentals=0
        ),
    )(*args)


def lookup_kernel(capacity, mixed, slot_ref, answer_ref, out_ref):
    slots = slot_ref[...]
    clusters = answer_ref.shape[0]
    shift = capacity.bit_length() - 1
    place = lax.bitwise_and(slots, capacity - 1)
    which = lax.shift_right_logical(slots, shift)
    if mixed:
        which = lax.bitwise_xor(which, lax.axis_index("owners") // 2)
    rows = slots.shape[1]
    pick = (lax.broadcasted_iota(jnp.int32, (capacity, rows), 0) == place).astype(jnp.float32).astype(jnp.bfloat16)
    rest = answer_ref[...]
    total = jnp.zeros((clusters, rows), jnp.float32)
    for _ in range(3):
        part = rest.astype(jnp.bfloat16)
        rest = rest - part.astype(jnp.float32)
        total = total + jnp.dot(part, pick, preferred_element_type=jnp.float32)
    mine = lax.broadcasted_iota(jnp.int32, (clusters, rows), 0) == which
    found = jnp.sum(jnp.where(mine, total, 0.0), axis=0, keepdims=True)
    out_ref[...] = jnp.maximum(found, -1.0).reshape(out_ref.shape)


def lookup(slots, answers, capacity, mixed):
    return pl.pallas_call(
        functools.partial(lookup_kernel, capacity, mixed),
        in_specs=[pl.BlockSpec(memory_space=pltpu.VMEM)] * 2,
        out_specs=pl.BlockSpec(memory_space=pltpu.VMEM),
        out_shape=jax.ShapeDtypeStruct((slots.shape[1],), jnp.float32),
        compiler_params=pltpu.CompilerParams(vmem_limit_bytes=VMEM_LIMIT),
    )(slots, answers)


def by_xor(value, axis, mask):
    return lax.ppermute(value, axis, [(source, source ^ mask) for source in range(lax.axis_size(axis))])


def after(value, *before):
    return lax.optimization_barrier((value, *before))[0]


def on_device(embeddings, cluster_of):
    owners = lax.axis_size("owners")
    clusters = owners // 2
    capacity = SLOTS // clusters
    rows = embeddings.shape[0]
    cluster_row = cluster_of.reshape(1, rows)
    same_core = [list(range(core, owners, 2)) for core in range(2)]
    mixed = clusters == 8
    if mixed:
        send = lambda block, mask: by_xor(block, "owners", 2 * mask)
        swap = lambda block: by_xor(block, "owners", 1)
        (out4, out5), slots = pack(cluster_row, embeddings, 4, [1, 1], clusters, capacity, mixed)
        far4, far5 = send(out4, 4), send(out5, 5)
        (own, out1, out2, out3), _ = pack(cluster_row, embeddings, 0, [1] * 4, clusters, capacity, mixed)
        (out6, out7), _ = pack(cluster_row, embeddings, 6, [1] * 2, clusters, capacity, mixed)
        near = [own, send(out1, 1), send(out2, 2), send(out3, 3)]
        far6 = send(after(out6, far4), 6)
        far7 = send(after(out7, far5), 7)
        early = [*near, far4, far5]
        early_other = [swap(block) for block in early]
        early_best = score(early, early_other)
        late = [far6, after(far7, early_best)]
        late_other = [swap(block) for block in late]
        best = score(early + late, early_other + late_other, 6, early_best, mixed)
    else:
        (outgoing,), slots = pack(cluster_row, embeddings, 0, [clusters], clusters, capacity, mixed)
        own = lax.all_to_all(
            outgoing.reshape(clusters, capacity, -1), "owners", 0, 0, axis_index_groups=same_core, tiled=True
        ).reshape(SLOTS, -1)
        best = score([own], [by_xor(own, "owners", 1)]).reshape(clusters, capacity)
    answers = lax.all_to_all(best, "owners", 0, 0, axis_index_groups=same_core, tiled=True)
    return lookup(slots, answers, capacity, mixed)


def solution(mesh):
    placed = (P(("groups", "owners"), None), P(("groups", "owners")))
    return jax.shard_map(
        on_device, mesh=mesh, in_specs=placed, out_specs=P(("groups", "owners")), check_vma=False
    )
```

time: 61.1 us -> 65.4 us (1.070)
  blocking collectives: 11.2 us -> 15.7 us
  other arithmetic: 1.47 us -> 0 us
  starting transfers between devices: 14.5 us -> 15.3 us
  Pallas kernels: 8 us -> 8.66 us
    all_to_all x1, blocking collectives: 11.2 us -> 15.7 us  [on_device(): lax.all_to_all(best, 'owners', 0, 0, axis_index_groups=same_core, tiled=T...]
    gather x2 -> x0, local copies, waits for them, and re-layouts: 1.11 us -> none  [the longest x1 0.56 us: on_device(): best = jnp.take(best, order, axis=0)]
    ppermute x15, starting transfers between devices: 14.5 us -> 15.3 us  [by_xor(): lax.ppermute(value, axis, [(source, source ^ mask) for source in range(la...]
    xor x1 -> x0, other arithmetic: 0.69 us -> none  [on_device(): relative = cluster_row ^ chip]
    reshape x0 -> x1, local copies, waits for them, and re-layouts: none -> 0.69 us  [on_device(): cluster_row = cluster_of.reshape(1, rows)]
    pallas_call x6, Pallas kernels: 8 us -> 8.66 us  [the longest x3 4.09 us: pack(): pl.pallas_call(functools.partial(pack_kernel, first_block, mixed, cluster...]
  transfers between devices with their start and end apart: 15 -> 15, of which waited for: 5 -> 7; matrix products, arithmetic and copies ran while one was open for 0% -> 0% of each run, Pallas kernels for 5% -> 8%
where the time goes in v2:
time: 65.4 us; the launch traced here: 65.2 us
  waiting for transfers between devices  23.1 us (35%)
  blocking collectives  15.7 us (24%)
  starting transfers between devices  15.3 us (23%)
  Pallas kernels  8.66 us (13%)
  local copies, waits for them, and re-layouts  2.35 us (4%)
    ppermute x15, waiting for transfers between devices, by_xor(): lax.ppermute(value, axis, [(source, source ^ mask) for source in range(la...  23.1 us
    all_to_all x1, blocking collectives, on_device(): lax.all_to_all(best, 'owners', 0, 0, axis_index_groups=same_core, tiled=T...  15.7 us
    ppermute x15, starting transfers between devices, by_xor(): lax.ppermute(value, axis, [(source, source ^ mask) for source in range(la...  15.3 us
    pallas_call x3, Pallas kernels, pack(): pl.pallas_call(functools.partial(pack_kernel, first_block, mixed, cluster...  4.09 us
    pallas_call x2, Pallas kernels, score(): pl.pallas_call(functools.partial(score_kernel, len(own), len(other), n_ol...  3.78 us
    unnamed x2, local copies, waits for them, and re-layouts  1.66 us
  transfers between devices with their start and end apart: 15, of which 7 were waited for; matrix products, arithmetic and copies ran while one was open for 0% of the time, Pallas kernels for 8%

profile of v2, /device:TPU:0, one launch (start us, length us, event | category | flops | bytes accessed | tf_op | source)
XLA Modules:
  0.0 65.2 jit_solution(12554738200680140965)
XLA Ops:
  0.0 0.7 %reshape.5.cluster_ref = s32[1,768]{1,0:T(1,128)S(1)} reshape(s32[768]{0:T(1024)} %param.3) | data formatting | bytes 6144 | tf_op jit(solution)/shard_map/reshape | solution.py:230
  0.7 0.0 copy-start
  0.7 1.7 %copy-done = f32[768,768]{1,0:T(8,128)S(1)} copy-done((f32[768,768]{1,0:T(8,128)S(1)}, f32[768,768]{1,0:T(8,128)}, u32[]{:S(2)}) %copy-start) | copy-done | bytes 2359320
  2.4 1.2 %shard_map.28 = (bf16[128,768]{1,0:T(8,128)(2,1)S(1)}, bf16[128,768]{1,0:T(8,128)(2,1)S(1)}, s32[1,768]{1,0:T(1,128)S(1)}) custom-call(s32[1,768]{1,0:T(1,128)S(1)} %reshape.5.cluster_ref, f32[768,768]{1,0:T(8,128)S(1)} %copy-done), custom_call_target="tpu_custom_call" | custom-call | flops 301989888 | bytes 2752512 | tf_op jit(solution)/shard_map/pallas_call | solution.py:79
  3.5 4.1 %collective-permute-start.3 = (bf16[128,768]{1,0:T(8,128)(2,1)S(1)}, bf16[128,768]{1,0:T(8,128)(2,1)S(1)}, u32[]{:S(2)}, u32[]{:S(2)}) collective-permute-start(bf16[128,768]{1,0:T(8,128)(2,1)S(1)} %get-tuple-element.22), channel_id=1, source_target_pairs={{0,8},{1,9},{2,10},{3,11},{4,12},{5,13},{6,14},{7,15},{8,0},{9,1},... | collective-permute-start | bytes 589832 | tf_op jit(solution)/shard_map/ppermute | solution.py:218
  7.6 1.3 %collective-permute-start.4 = (bf16[128,768]{1,0:T(8,128)(2,1)S(1)}, bf16[128,768]{1,0:T(8,128)(2,1)S(1)}, u32[]{:S(2)}, u32[]{:S(2)}) collective-permute-start(bf16[128,768]{1,0:T(8,128)(2,1)S(1)} %get-tuple-element.23), channel_id=1, source_target_pairs={{0,10},{1,11},{2,8},{3,9},{4,14},{5,15},{6,12},{7,13},{8,2},{9,3},... | collective-permute-start | bytes 589832 | tf_op jit(solution)/shard_map/ppermute | solution.py:218
  8.9 1.7 %shard_map.29 = (bf16[128,768]{1,0:T(8,128)(2,1)S(1)}, bf16[128,768]{1,0:T(8,128)(2,1)S(1)}, bf16[128,768]{1,0:T(8,128)(2,1)S(1)}, bf16[128,768]{1,0:T(8,128)(2,1)S(1)}, s32[1,768]{1,0:T(1,128)}) custom-call(s32[1,768]{1,0:T(1,128)S(1)} %reshape.5.cluster_ref, f32[768,768]{1,0:T(8,128)S(1)} %copy-done), custom_call_target="tpu_custom_call" | custom-call | flops 603979776 | bytes 3145728 | tf_op jit(solution)/shard_map/pallas_call | solution.py:79
  10.6 0.3 collective-permute-start
  10.9 1.8 %collective-permute-start.1 = (bf16[128,768]{1,0:T(8,128)(2,1)S(1)}, bf16[128,768]{1,0:T(8,128)(2,1)S(1)}, u32[]{:S(2)}, u32[]{:S(2)}) collective-permute-start(bf16[128,768]{1,0:T(8,128)(2,1)S(1)} %get-tuple-element.20), channel_id=1, source_target_pairs={{0,4},{1,5},{2,6},{3,7},{4,0},{5,1},{6,2},{7,3},{8,12},{9,13},{10,... | collective-permute-start | bytes 589832 | tf_op jit(solution)/shard_map/ppermute | solution.py:218
  12.8 1.4 %collective-permute-start.2 = (bf16[128,768]{1,0:T(8,128)(2,1)S(1)}, bf16[128,768]{1,0:T(8,128)(2,1)S(1)}, u32[]{:S(2)}, u32[]{:S(2)}) collective-permute-start(bf16[128,768]{1,0:T(8,128)(2,1)S(1)} %get-tuple-element.21), channel_id=1, source_target_pairs={{0,6},{1,7},{2,4},{3,5},{4,2},{5,3},{6,0},{7,1},{8,14},{9,15},{10,... | collective-permute-start | bytes 589832 | tf_op jit(solution)/shard_map/ppermute | solution.py:218
  14.2 7.7 %collective-permute-done.3.refs_4_ = bf16[128,768]{1,0:T(8,128)(2,1)S(1)} collective-permute-done((bf16[128,768]{1,0:T(8,128)(2,1)S(1)}, bf16[128,768]{1,0:T(8,128)(2,1)S(1)}, u32[]{:S(2)}, u32[]{:S(2)}) %collective-permute-start.3) | collective-permute-done | bytes 196640 | tf_op jit(solution)/shard_map/ppermute | solution.py:218
  21.9 0.0 collective-permute-start.7
  21.9 4.4 %collective-permute-done.4.refs_5_ = bf16[128,768]{1,0:T(8,128)(2,1)S(1)} collective-permute-done((bf16[128,768]{1,0:T(8,128)(2,1)S(1)}, bf16[128,768]{1,0:T(8,128)(2,1)S(1)}, u32[]{:S(2)}, u32[]{:S(2)}) %collective-permute-start.4) | collective-permute-done | bytes 196640 | tf_op jit(solution)/shard_map/ppermute | solution.py:218
  26.3 0.0 collective-permute-start.11
  26.3 0.0 collective-permute-done.refs_1_
  26.3 0.5 collective-permute-start.12
  26.8 0.0 collective-permute-done.1.refs_2_
  26.8 0.1 collective-permute-start.8
  26.9 2.6 %collective-permute-done.2.refs_3_ = bf16[128,768]{1,0:T(8,128)(2,1)S(1)} collective-permute-done((bf16[128,768]{1,0:T(8,128)(2,1)S(1)}, bf16[128,768]{1,0:T(8,128)(2,1)S(1)}, u32[]{:S(2)}, u32[]{:S(2)}) %collective-permute-start.2) | collective-permute-done | bytes 196640 | tf_op jit(solution)/shard_map/ppermute | solution.py:218
  29.5 0.0 collective-permute-start.9
  29.5 0.0 collective-permute-done.7.refs_6_.refs_8_
  29.5 0.5 collective-permute-start.10
  30.0 1.2 %shard_map.30 = (bf16[128,768]{1,0:T(8,128)(2,1)S(1)}, bf16[128,768]{1,0:T(8,128)(2,1)S(1)}, s32[1,768]{1,0:T(1,128)}) custom-call(s32[1,768]{1,0:T(1,128)S(1)} %reshape.5.cluster_ref, f32[768,768]{1,0:T(8,128)S(1)} %copy-done), custom_call_target="tpu_custom_call" | custom-call | flops 301989888 | bytes 2752512 | tf_op jit(solution)/shard_map/pallas_call | solution.py:79
  31.2 0.0 collective-permute-done.11.refs_10_.refs_12_
  31.3 4.6 %collective-permute-start.6 = (bf16[128,768]{1,0:T(8,128)(2,1)S(1)}, bf16[128,768]{1,0:T(8,128)(2,1)S(1)}, u32[]{:S(2)}, u32[]{:S(2)}) collective-permute-start(bf16[128,768]{1,0:T(8,128)(2,1)S(1)} %get-tuple-element.27), channel_id=1, source_target_pairs={{0,14},{1,15},{2,12},{3,13},{4,10},{5,11},{6,8},{7,9},{8,6},{9,7},... | collective-permute-start | bytes 589832 | tf_op jit(solution)/shard_map/ppermute | solution.py:218
  35.9 0.0 collective-permute-done.12.refs_11_.refs_13_
  35.9 0.1 collective-permute-start.5
  36.0 0.0 collective-permute-done.8.refs_7_.refs_9_
  36.0 0.0 collective-permute-done.9.refs_8_.refs_10_
  36.0 0.0 collective-permute-done.10.refs_9_.refs_11_
  36.0 2.1 %shard_map.31.refs_16_ = f32[6,128]{1,0:T(8,128)S(1)} custom-call(bf16[128,768]{1,0:T(8,128)(2,1)S(1)} %get-tuple-element.18.refs_0_, bf16[128,768]{1,0:T(8,128)(2,1)S(1)} %collective-permute-done.refs_1_, bf16[128,768]{1,0:T(8,128)(2,1)S(1)} %collective-permute-done.1.refs_2_, bf16[128,768]{1,0:T(8,128)(2,1)S(1)} %collective-permute-done.2.refs_3_, ...), custom_call_target="tpu_custom_call" | custom-call | flops 1811939328 | bytes 2359296 | tf_op jit(solution)/shard_map/pallas_call | solution.py:174
  38.1 3.1 %collective-permute-done.6.refs_7_ = bf16[128,768]{1,0:T(8,128)(2,1)S(1)} collective-permute-done((bf16[128,768]{1,0:T(8,128)(2,1)S(1)}, bf16[128,768]{1,0:T(8,128)(2,1)S(1)}, u32[]{:S(2)}, u32[]{:S(2)}) %collective-permute-start.6) | collective-permute-done | bytes 196640 | tf_op jit(solution)/shard_map/ppermute | solution.py:218
  41.2 4.1 %collective-permute-done.5.refs_6_ = bf16[128,768]{1,0:T(8,128)(2,1)S(1)} collective-permute-done((bf16[128,768]{1,0:T(8,128)(2,1)S(1)}, bf16[128,768]{1,0:T(8,128)(2,1)S(1)}, u32[]{:S(2)}, u32[]{:S(2)}) %collective-permute-start.5) | collective-permute-done | bytes 196640 | tf_op jit(solution)/shard_map/ppermute | solution.py:218
  45.3 0.0 collective-permute-start.13
  45.3 0.5 collective-permute-start.14
  45.8 0.9 %collective-permute-done.13.refs_14_ = bf16[128,768]{1,0:T(8,128)(2,1)S(1)} collective-permute-done((bf16[128,768]{1,0:T(8,128)(2,1)S(1)}, bf16[128,768]{1,0:T(8,128)(2,1)S(1)}, u32[]{:S(2)}, u32[]{:S(2)}) %collective-permute-start.13) | collective-permute-done | bytes 196640 | tf_op jit(solution)/shard_map/ppermute | solution.py:218
  46.7 0.3 collective-permute-done.14.refs_15_
  47.0 1.7 %shard_map.32 = f32[8,128]{1,0:T(8,128)S(1)} custom-call(bf16[128,768]{1,0:T(8,128)(2,1)S(1)} %get-tuple-element.18.refs_0_, bf16[128,768]{1,0:T(8,128)(2,1)S(1)} %collective-permute-done.refs_1_, bf16[128,768]{1,0:T(8,128)(2,1)S(1)} %collective-permute-done.1.refs_2_, bf16[128,768]{1,0:T(8,128)(2,1)S(1)} %collective-permute-done.2.refs_3_, ...), custom_call_target="tpu_custom_call" | custom-call | flops 3221225472 | bytes 3145728 | tf_op jit(solution)/shard_map/pallas_call | solution.py:174
  48.7 15.7 %all_to_all.11 = f32[8,1,128]{2,1,0:T(1,128)S(1)} all-to-all(f32[8,1,128]{2,1,0:T(1,128)S(1)} %bitcast.5), channel_id=1, replica_groups={{0,2,4,6,8,10,12,14},{1,3,5,7,9,11,13,15},{16,18,20,22,24,26,28,30},{17..., dimensions={0} | all-to-all | bytes 8192 | tf_op jit(solution)/shard_map/all_to_all | solution.py:255
  64.4 0.8 %shard_map.33 = f32[768]{0:T(1024)} custom-call(s32[1,768]{1,0:T(1,128)S(1)} %get-tuple-element.17.slot_ref, f32[8,128]{1,0:T(8,128)S(1)} %bitcast.4), custom_call_target="tpu_custom_call" | custom-call | tf_op jit(solution)/shard_map/pallas_call | solution.py:208
Async XLA Ops:
  0.7 1.7 %copy-start = (f32[768,768]{1,0:T(8,128)S(1)}, f32[768,768]{1,0:T(8,128)}, u32[]{:S(2)}) copy-start(f32[768,768]{1,0:T(8,128)} %rows_ref.5) | copy-start | bytes 7077892
  3.5 18.4 %collective-permute-start.3 = (bf16[128,768]{1,0:T(8,128)(2,1)S(1)}, bf16[128,768]{1,0:T(8,128)(2,1)S(1)}, u32[]{:S(2)}, u32[]{:S(2)}) collective-permute-start(bf16[128,768]{1,0:T(8,128)(2,1)S(1)} %get-tuple-element.22), channel_id=1, source_target_pairs={{0,8},{1,9},{2,10},{3,11},{4,12},{5,13},{6,14},{7,15},{8,0},{9,1},... | collective-permute-start | bytes 589832 | tf_op jit(solution)/shard_map/ppermute | solution.py:218
  7.6 18.6 %collective-permute-start.4 = (bf16[128,768]{1,0:T(8,128)(2,1)S(1)}, bf16[128,768]{1,0:T(8,128)(2,1)S(1)}, u32[]{:S(2)}, u32[]{:S(2)}) collective-permute-start(bf16[128,768]{1,0:T(8,128)(2,1)S(1)} %get-tuple-element.23), channel_id=1, source_target_pairs={{0,10},{1,11},{2,8},{3,9},{4,14},{5,15},{6,12},{7,13},{8,2},{9,3},... | collective-permute-start | bytes 589832 | tf_op jit(solution)/shard_map/ppermute | solution.py:218
  10.6 15.7 %collective-permute-start = (bf16[128,768]{1,0:T(8,128)(2,1)S(1)}, bf16[128,768]{1,0:T(8,128)(2,1)S(1)}, u32[]{:S(2)}, u32[]{:S(2)}) collective-permute-start(bf16[128,768]{1,0:T(8,128)(2,1)S(1)} %get-tuple-element.19), channel_id=1, source_target_pairs={{0,2},{1,3},{2,0},{3,1},{4,6},{5,7},{6,4},{7,5},{8,10},{9,11},{10,... | collective-permute-start | bytes 589832 | tf_op jit(solution)/shard_map/ppermute | solution.py:218
  10.9 15.9 %collective-permute-start.1 = (bf16[128,768]{1,0:T(8,128)(2,1)S(1)}, bf16[128,768]{1,0:T(8,128)(2,1)S(1)}, u32[]{:S(2)}, u32[]{:S(2)}) collective-permute-start(bf16[128,768]{1,0:T(8,128)(2,1)S(1)} %get-tuple-element.20), channel_id=1, source_target_pairs={{0,4},{1,5},{2,6},{3,7},{4,0},{5,1},{6,2},{7,3},{8,12},{9,13},{10,... | collective-permute-start | bytes 589832 | tf_op jit(solution)/shard_map/ppermute | solution.py:218
  12.8 16.7 %collective-permute-start.2 = (bf16[128,768]{1,0:T(8,128)(2,1)S(1)}, bf16[128,768]{1,0:T(8,128)(2,1)S(1)}, u32[]{:S(2)}, u32[]{:S(2)}) collective-permute-start(bf16[128,768]{1,0:T(8,128)(2,1)S(1)} %get-tuple-element.21), channel_id=1, source_target_pairs={{0,6},{1,7},{2,4},{3,5},{4,2},{5,3},{6,0},{7,1},{8,14},{9,15},{10,... | collective-permute-start | bytes 589832 | tf_op jit(solution)/shard_map/ppermute | solution.py:218
  21.9 7.6 %collective-permute-start.7 = (bf16[128,768]{1,0:T(8,128)(2,1)S(1)}, bf16[128,768]{1,0:T(8,128)(2,1)S(1)}, u32[]{:S(2)}, u32[]{:S(2)}) collective-permute-start(bf16[128,768]{1,0:T(8,128)(2,1)S(1)} %get-tuple-element.18.refs_0_), channel_id=1, source_target_pairs={{0,1},{1,0},{2,3},{3,2},{4,5},{5,4},{6,7},{7,6},{8,9},{9,8},{10,11... | collective-permute-start | bytes 589832 | tf_op jit(solution)/shard_map/ppermute | solution.py:218
  26.3 5.0 %collective-permute-start.11 = (bf16[128,768]{1,0:T(8,128)(2,1)S(1)}, bf16[128,768]{1,0:T(8,128)(2,1)S(1)}, u32[]{:S(2)}, u32[]{:S(2)}) collective-permute-start(bf16[128,768]{1,0:T(8,128)(2,1)S(1)} %collective-permute-done.3.refs_4_), channel_id=1, source_target_pairs={{0,1},{1,0},{2,3},{3,2},{4,5},{5,4},{6,7},{7,6},{8,9},{9,8},{10,11... | collective-permute-start | bytes 589832 | tf_op jit(solution)/shard_map/ppermute | solution.py:218
  26.3 9.6 %collective-permute-start.12 = (bf16[128,768]{1,0:T(8,128)(2,1)S(1)}, bf16[128,768]{1,0:T(8,128)(2,1)S(1)}, u32[]{:S(2)}, u32[]{:S(2)}) collective-permute-start(bf16[128,768]{1,0:T(8,128)(2,1)S(1)} %collective-permute-done.4.refs_5_), channel_id=1, source_target_pairs={{0,1},{1,0},{2,3},{3,2},{4,5},{5,4},{6,7},{7,6},{8,9},{9,8},{10,11... | collective-permute-start | bytes 589832 | tf_op jit(solution)/shard_map/ppermute | solution.py:218
  26.8 9.2 %collective-permute-start.8 = (bf16[128,768]{1,0:T(8,128)(2,1)S(1)}, bf16[128,768]{1,0:T(8,128)(2,1)S(1)}, u32[]{:S(2)}, u32[]{:S(2)}) collective-permute-start(bf16[128,768]{1,0:T(8,128)(2,1)S(1)} %collective-permute-done.refs_1_), channel_id=1, source_target_pairs={{0,1},{1,0},{2,3},{3,2},{4,5},{5,4},{6,7},{7,6},{8,9},{9,8},{10,11... | collective-permute-start | bytes 589832 | tf_op jit(solution)/shard_map/ppermute | solution.py:218
  29.5 6.5 %collective-permute-start.9 = (bf16[128,768]{1,0:T(8,128)(2,1)S(1)}, bf16[128,768]{1,0:T(8,128)(2,1)S(1)}, u32[]{:S(2)}, u32[]{:S(2)}) collective-permute-start(bf16[128,768]{1,0:T(8,128)(2,1)S(1)} %collective-permute-done.1.refs_2_), channel_id=1, source_target_pairs={{0,1},{1,0},{2,3},{3,2},{4,5},{5,4},{6,7},{7,6},{8,9},{9,8},{10,11... | collective-permute-start | bytes 589832 | tf_op jit(solution)/shard_map/ppermute | solution.py:218
  29.5 6.5 %collective-permute-start.10 = (bf16[128,768]{1,0:T(8,128)(2,1)S(1)}, bf16[128,768]{1,0:T(8,128)(2,1)S(1)}, u32[]{:S(2)}, u32[]{:S(2)}) collective-permute-start(bf16[128,768]{1,0:T(8,128)(2,1)S(1)} %collective-permute-done.2.refs_3_), channel_id=1, source_target_pairs={{0,1},{1,0},{2,3},{3,2},{4,5},{5,4},{6,7},{7,6},{8,9},{9,8},{10,11... | collective-permute-start | bytes 589832 | tf_op jit(solution)/shard_map/ppermute | solution.py:218
  31.3 9.9 %collective-permute-start.6 = (bf16[128,768]{1,0:T(8,128)(2,1)S(1)}, bf16[128,768]{1,0:T(8,128)(2,1)S(1)}, u32[]{:S(2)}, u32[]{:S(2)}) collective-permute-start(bf16[128,768]{1,0:T(8,128)(2,1)S(1)} %get-tuple-element.27), channel_id=1, source_target_pairs={{0,14},{1,15},{2,12},{3,13},{4,10},{5,11},{6,8},{7,9},{8,6},{9,7},... | collective-permute-start | bytes 589832 | tf_op jit(solution)/shard_map/ppermute | solution.py:218
  35.9 9.4 %collective-permute-start.5 = (bf16[128,768]{1,0:T(8,128)(2,1)S(1)}, bf16[128,768]{1,0:T(8,128)(2,1)S(1)}, u32[]{:S(2)}, u32[]{:S(2)}) collective-permute-start(bf16[128,768]{1,0:T(8,128)(2,1)S(1)} %get-tuple-element.25), channel_id=1, source_target_pairs={{0,12},{1,13},{2,14},{3,15},{4,8},{5,9},{6,10},{7,11},{8,4},{9,5},... | collective-permute-start | bytes 589832 | tf_op jit(solution)/shard_map/ppermute | solution.py:218
  45.3 1.4 %collective-permute-start.13 = (bf16[128,768]{1,0:T(8,128)(2,1)S(1)}, bf16[128,768]{1,0:T(8,128)(2,1)S(1)}, u32[]{:S(2)}, u32[]{:S(2)}) collective-permute-start(bf16[128,768]{1,0:T(8,128)(2,1)S(1)} %collective-permute-done.5.refs_6_), channel_id=1, source_target_pairs={{0,1},{1,0},{2,3},{3,2},{4,5},{5,4},{6,7},{7,6},{8,9},{9,8},{10,11... | collective-permute-start | bytes 589832 | tf_op jit(solution)/shard_map/ppermute | solution.py:218
  45.3 1.7 %collective-permute-start.14 = (bf16[128,768]{1,0:T(8,128)(2,1)S(1)}, bf16[128,768]{1,0:T(8,128)(2,1)S(1)}, u32[]{:S(2)}, u32[]{:S(2)}) collective-permute-start(bf16[128,768]{1,0:T(8,128)(2,1)S(1)} %collective-permute-done.6.refs_7_), channel_id=1, source_target_pairs={{0,1},{1,0},{2,3},{3,2},{4,5},{5,4},{6,7},{7,6},{8,9},{9,8},{10,11... | collective-permute-start | bytes 589832 | tf_op jit(solution)/shard_map/ppermute | solution.py:218

commit v3 on v2

v3 whole, which is shorter than its diff:
```python
import functools

import jax
import jax.numpy as jnp
from jax import lax
from jax.experimental import pallas as pl
from jax.experimental.pallas import tpu as pltpu
from jax.sharding import PartitionSpec as P

SLOTS = 1024
FLOOR = -4.0
DEAD = 4.0
VMEM_LIMIT = 40 * 2**20
LANES = 128


def row_slots(relative, clusters, capacity):
    rows = relative.shape[1]
    ids = lax.broadcasted_iota(jnp.int32, (clusters, LANES), 0)
    earlier = (
        lax.broadcasted_iota(jnp.int32, (LANES, LANES), 0)
        < lax.broadcasted_iota(jnp.int32, (LANES, LANES), 1)
    ).astype(jnp.bfloat16)
    carry = jnp.zeros((clusters, 1), jnp.float32)
    places = []
    for first in range(0, rows, LANES):
        part = relative[:, first : first + LANES]
        member = (ids == part).astype(jnp.float32)
        before = carry + jnp.dot(
            member.astype(jnp.bfloat16), earlier, preferred_element_type=jnp.float32
        )
        place = jnp.sum(before * member, axis=0, keepdims=True)
        places.append(part * capacity + place.astype(jnp.int32))
        carry = carry + jnp.sum(member, axis=1, keepdims=True)
    return jnp.concatenate(places, axis=1), carry


def picks(slots, taken, capacity, pick_ref):
    done = 0
    for first, count in taken:
        size = count * capacity
        wanted = lax.broadcasted_iota(jnp.int32, (size, slots.shape[1]), 0) + first * capacity
        pick_ref[done : done + size, :] = (wanted == slots).astype(jnp.float32).astype(jnp.bfloat16)
        done += size


def select(taken, capacity, counts, pick_ref, unit_ref, block_refs):
    lane = lax.broadcasted_iota(jnp.int32, (capacity, LANES), 1)
    place = lax.broadcasted_iota(jnp.int32, (capacity, LANES), 0).astype(jnp.float32)
    done = 0
    for block_ref, (first, count) in zip(block_refs, taken):
        for index in range(count):
            block = jnp.dot(
                pick_ref[done : done + capacity, :], unit_ref[...], preferred_element_type=jnp.float32
            )
            full = counts[first + index : first + index + 1, :]
            mark = jnp.where((place >= full) & (lane == 0), DEAD, 0.0)
            start = index * capacity
            block_ref[start : start + capacity, :LANES] = (block[:, :LANES] + mark).astype(jnp.bfloat16)
            block_ref[start : start + capacity, LANES:] = block[:, LANES:].astype(jnp.bfloat16)
            done += capacity


def pack_kernel(taken, mixed, clusters, capacity, cluster_ref, rows_ref, *refs):
    *block_refs, slot_ref, count_ref, unit_ref, ids_ref, held_ref, pick_ref, sems = refs
    steps, tile, _ = held_ref.shape
    ids_copy = pltpu.make_async_copy(cluster_ref, ids_ref, sems.at[steps])
    ids_copy.start()
    copies = [
        pltpu.make_async_copy(rows_ref.at[pl.ds(step * tile, tile), :], held_ref.at[step], sems.at[step])
        for step in range(steps)
    ]
    for copy in copies:
        copy.start()
    ids_copy.wait()
    relative = ids_ref[...].reshape(1, steps * tile)
    if mixed:
        relative = lax.bitwise_xor(relative, lax.axis_index("owners") // 2)
    slots, counts = row_slots(relative, clusters, capacity)
    slot_ref[...] = slots
    count_ref[...] = jnp.broadcast_to(counts, count_ref.shape)
    picks(slots, taken, capacity, pick_ref)
    for step, copy in enumerate(copies):
        copy.wait()
        values = held_ref[step]
        scale = lax.rsqrt(jnp.sum(values * values, axis=1, keepdims=True) + 1e-06)
        unit_ref[step * tile : (step + 1) * tile, :] = (values * scale).astype(jnp.bfloat16)
    select(taken, capacity, counts, pick_ref, unit_ref, block_refs)


def pack_cost(taken, capacity, rows, width):
    total = sum(count for _, count in taken) * capacity
    return pl.CostEstimate(
        flops=2 * total * rows * width, bytes_accessed=rows * width * 4 + total * width * 2, transcendentals=rows
    )


def block_shapes(taken, capacity, width):
    return [jax.ShapeDtypeStruct((count * capacity, width), jnp.bfloat16) for _, count in taken]


def pack(cluster_of, embeddings, taken, clusters, capacity, mixed):
    rows, width = embeddings.shape
    steps = 3 if rows % 384 == 0 else 1
    total = sum(count for _, count in taken) * capacity
    vmem = pl.BlockSpec(memory_space=pltpu.VMEM)
    *blocks, slots, counts, unit = pl.pallas_call(
        functools.partial(pack_kernel, taken, mixed, clusters, capacity),
        in_specs=[pl.BlockSpec(memory_space=pl.ANY)] * 2,
        out_specs=[vmem] * (len(taken) + 3),
        out_shape=block_shapes(taken, capacity, width)
        + [
            jax.ShapeDtypeStruct((1, rows), jnp.int32),
            jax.ShapeDtypeStruct((clusters, LANES), jnp.float32),
            jax.ShapeDtypeStruct((rows, width), jnp.bfloat16),
        ],
        scratch_shapes=[
            pltpu.VMEM((rows,), jnp.int32),
            pltpu.VMEM((steps, rows // steps, width), jnp.float32),
            pltpu.VMEM((total, rows), jnp.bfloat16),
            pltpu.SemaphoreType.DMA((steps + 1,)),
        ],
        compiler_params=pltpu.CompilerParams(vmem_limit_bytes=VMEM_LIMIT),
        cost_estimate=pack_cost(taken, capacity, rows, width),
    )(
        pltpu.with_memory_space_constraint(cluster_of, pltpu.HBM),
        pltpu.with_memory_space_constraint(embeddings, pltpu.HBM),
    )
    return blocks, (slots, counts, unit)


def more_kernel(taken, capacity, slot_ref, count_ref, unit_ref, *refs):
    *block_refs, pick_ref = refs
    picks(slot_ref[...], taken, capacity, pick_ref)
    select(taken, capacity, count_ref[...], pick_ref, unit_ref, block_refs)


def pack_more(packed, taken, capacity):
    rows, width = packed[2].shape
    total = sum(count for _, count in taken) * capacity
    vmem = pl.BlockSpec(memory_space=pltpu.VMEM)
    return pl.pallas_call(
        functools.partial(more_kernel, taken, capacity),
        in_specs=[vmem] * 3,
        out_specs=[vmem] * len(taken),
        out_shape=block_shapes(taken, capacity, width),
        scratch_shapes=[pltpu.VMEM((total, rows), jnp.bfloat16)],
        compiler_params=pltpu.CompilerParams(vmem_limit_bytes=VMEM_LIMIT),
        cost_estimate=pack_cost(taken, capacity, rows, width),
    )(*packed)


def pieces(refs, tile):
    groups, current, held = [], [], 0
    for ref in refs:
        start = 0
        while start < ref.shape[0]:
            size = min(tile - held, ref.shape[0] - start)
            current.append((ref, start, size))
            start += size
            held += size
            if held == tile:
                groups.append(current)
                current, held = [], 0
    if current:
        groups.append(current)
    return groups


def load(group):
    parts = [ref[start : start + size, :] for ref, start, size in group]
    return parts[0] if len(parts) == 1 else jnp.concatenate(parts, axis=0)


def tile_best(key, query, shift):
    deep, wide = key.shape[0], query.shape[0]
    scores = lax.dot_general(key, query, (((1,), (1,)), ((), ())), preferred_element_type=jnp.float32)
    dead = key[:, :1].astype(jnp.float32) > 2.0
    scores = scores + jnp.where(dead, 2 * FLOOR, 0.0)
    if shift is not None and -wide < shift < deep:
        own = lax.broadcasted_iota(jnp.int32, scores.shape, 0) == (
            lax.broadcasted_iota(jnp.int32, scores.shape, 1) + shift
        )
        scores = jnp.where(own, FLOOR, scores)
    return jnp.max(scores.reshape(deep // 8, 8, wide), axis=0)


def score_kernel(plan, n_blocks, has_start, order, *refs):
    start_ref = refs[n_blocks] if has_start else None
    best_ref = refs[-1]
    chip = lax.axis_index("owners") // 2 if order else 0
    at = 0
    for query_block, key_blocks, starts in plan:
        first = 0
        for query_group in pieces([refs[query_block]], 256):
            query = load(query_group)
            wide = query.shape[0]
            best = jnp.full((8, wide), FLOOR, jnp.float32)
            for key_block in key_blocks:
                key_first = 0
                for key_group in pieces([refs[key_block]], 512):
                    key = load(key_group)
                    shift = first - key_first if key_block == query_block else None
                    best = jnp.maximum(best, tile_best(key, query, shift))
                    key_first += key.shape[0]
            row = jnp.max(best, axis=0, keepdims=True)
            for lane in range(0, wide, LANES):
                index = (at + first + lane) // LANES
                part = row[:, lane : lane + LANES]
                if starts:
                    part = jnp.maximum(part, start_ref[index : index + 1, :])
                best_ref[pl.ds(lax.bitwise_xor(order[index], chip) if order else index, 1), :] = part
            first += wide
        at += first


def score(blocks, plan, start=None, order=None):
    n_query = sum(blocks[query].shape[0] for query, _, _ in plan)
    pairs = sum(blocks[query].shape[0] * blocks[key].shape[0] for query, keys, _ in plan for key in keys)
    width = blocks[0].shape[1]
    args = [*blocks] + ([] if start is None else [start])
    return pl.pallas_call(
        functools.partial(score_kernel, plan, len(blocks), start is not None, order),
        in_specs=[pl.BlockSpec(memory_space=pltpu.VMEM)] * len(args),
        out_specs=pl.BlockSpec(memory_space=pltpu.VMEM),
        out_shape=jax.ShapeDtypeStruct((n_query // LANES, LANES), jnp.float32),
        compiler_params=pltpu.CompilerParams(vmem_limit_bytes=VMEM_LIMIT),
        cost_estimate=pl.CostEstimate(
            flops=2 * pairs * width,
            bytes_accessed=sum(block.size for block in blocks) * 2,
            transcendentals=0,
        ),
    )(*args)


def lookup_kernel(capacity, mixed, slot_ref, answer_ref, out_ref):
    slots = slot_ref[...]
    clusters = answer_ref.shape[0]
    shift = capacity.bit_length() - 1
    place = lax.bitwise_and(slots, capacity - 1)
    which = lax.shift_right_logical(slots, shift)
    if mixed:
        which = lax.bitwise_xor(which, lax.axis_index("owners") // 2)
    rows = slots.shape[1]
    pick = (lax.broadcasted_iota(jnp.int32, (capacity, rows), 0) == place).astype(jnp.float32).astype(jnp.bfloat16)
    rest = answer_ref[...]
    total = jnp.zeros((clusters, rows), jnp.float32)
    for _ in range(3):
        part = rest.astype(jnp.bfloat16)
        rest = rest - part.astype(jnp.float32)
        total = total + jnp.dot(part, pick, preferred_element_type=jnp.float32)
    mine = lax.broadcasted_iota(jnp.int32, (clusters, rows), 0) == which
    found = jnp.sum(jnp.where(mine, total, 0.0), axis=0, keepdims=True)
    out_ref[...] = jnp.maximum(found, -1.0).reshape(out_ref.shape)


def lookup(slots, answers, capacity, mixed):
    return pl.pallas_call(
        functools.partial(lookup_kernel, capacity, mixed),
        in_specs=[pl.BlockSpec(memory_space=pltpu.VMEM)] * 2,
        out_specs=pl.BlockSpec(memory_space=pltpu.VMEM),
        out_shape=jax.ShapeDtypeStruct((slots.shape[1],), jnp.float32),
        compiler_params=pltpu.CompilerParams(vmem_limit_bytes=VMEM_LIMIT),
    )(slots, answers)


def by_xor(value, axis, mask):
    return lax.ppermute(value, axis, [(source, source ^ mask) for source in range(lax.axis_size(axis))])


def after(value, *before):
    return lax.optimization_barrier((value, *before))[0]


def on_device(embeddings, cluster_of):
    owners = lax.axis_size("owners")
    clusters = owners // 2
    capacity = SLOTS // clusters
    same_core = [list(range(core, owners, 2)) for core in range(2)]
    mixed = clusters == 8
    if mixed:
        send = lambda block, mask: by_xor(block, "owners", 2 * mask)
        swap = lambda block: by_xor(block, "owners", 1)
        first, then = (4, 5), (0, 1, 2, 3, 6, 7)
        blocks = {}
        got, packed = pack(cluster_of, embeddings, [(index, 1) for index in first], clusters, capacity, mixed)
        blocks.update(zip(first, got))
        blocks.update(zip(then, pack_more(packed, [(index, 1) for index in then], capacity)))
        waits = {6: (4,), 7: (5,)}
        have = {0: blocks[0]}
        for index in (4, 5, 1, 2, 3, 6, 7):
            have[index] = send(after(blocks[index], *[have[wait] for wait in waits.get(index, ())]), index)
        early = jnp.concatenate([have[index] for index in [0, 4, 5, 1]], axis=0)
        early_other = swap(early)
        best = score([early, early_other], [(0, [0, 1], False)])
        late = jnp.concatenate([have[index] for index in [2, 3, 6, 7]], axis=0)
        late_other = swap(late)
        best = score([early, late], [(0, [1], True), (1, [0, 1], False)], best)
        best = score(
            [early, late, early_other, late_other], [(0, [3], True), (1, [2, 3], True)], best, [0, 4, 5, 1, 2, 3, 6, 7]
        )
        slots = packed[0]
    else:
        (outgoing,), (slots, _, _) = pack(cluster_of, embeddings, [(0, clusters)], clusters, capacity, mixed)
        own = lax.all_to_all(
            outgoing.reshape(clusters, capacity, -1), "owners", 0, 0, axis_index_groups=same_core, tiled=True
        ).reshape(SLOTS, -1)
        other = by_xor(own, "owners", 1)
        best = score([own], [(0, [0], False)])
        best = score([own, other], [(0, [1], True)], best).reshape(clusters, capacity)
    answers = lax.all_to_all(best, "owners", 0, 0, axis_index_groups=same_core, tiled=True)
    return lookup(slots, answers, capacity, mixed)


def solution(mesh):
    placed = (P(("groups", "owners"), None), P(("groups", "owners")))
    return jax.shard_map(
        on_device, mesh=mesh, in_specs=placed, out_specs=P(("groups", "owners")), check_vma=False
    )
```

time: 65.4 us -> 57 us (0.87)
  waiting for transfers between devices: 23.1 us -> 19.2 us
  local copies, waits for them, and re-layouts: 2.35 us -> 0.12 us
  starting transfers between devices: 15.3 us -> 13.4 us
    ppermute x15 -> x9, waiting for transfers between devices: 23.1 us -> 19.2 us  [by_xor(): lax.ppermute(value, axis, [(source, source ^ mask) for source in range(la...]
    ppermute x15 -> x9, starting transfers between devices: 15.3 us -> 13.4 us  [by_xor(): lax.ppermute(value, axis, [(source, source ^ mask) for source in range(la...]
    unnamed x2 -> x6, local copies, waits for them, and re-layouts: 1.66 us -> 0.09 us
    reshape x1 -> x0, local copies, waits for them, and re-layouts: 0.69 us -> none  [on_device(): cluster_row = cluster_of.reshape(1, rows)]
  transfers between devices with their start and end apart: 15 -> 9, of which waited for: 7 -> 3; matrix products, arithmetic and copies ran while one was open for 0% -> 0% of each run, Pallas kernels for 8% -> 6%
where the time goes in v3:
time: 57 us; the launch traced here: 56.8 us
  waiting for transfers between devices  19.2 us (34%)
  blocking collectives  15.8 us (28%)
  starting transfers between devices  13.4 us (24%)
  Pallas kernels  8.07 us (14%)
    ppermute x9, waiting for transfers between devices, by_xor(): lax.ppermute(value, axis, [(source, source ^ mask) for source in range(la...  19.2 us
    all_to_all x1, blocking collectives, on_device(): lax.all_to_all(best, 'owners', 0, 0, axis_index_groups=same_core, tiled=T...  15.8 us
    ppermute x9, starting transfers between devices, by_xor(): lax.ppermute(value, axis, [(source, source ^ mask) for source in range(la...  13.4 us
    pallas_call x3, Pallas kernels, score(): pl.pallas_call(functools.partial(score_kernel, plan, len(blocks), start i...  3.95 us
    pallas_call x1, Pallas kernels, pack(): pl.pallas_call(functools.partial(pack_kernel, taken, mixed, clusters, cap...  2.21 us
  transfers between devices with their start and end apart: 9, of which 3 were waited for; matrix products, arithmetic and copies ran while one was open for 0% of the time, Pallas kernels for 6%

profile of v3, /device:TPU:0, one launch (start us, length us, event | category | flops | bytes accessed | tf_op | source)
XLA Modules:
  0.0 56.8 jit_solution(5883111883771737218)
XLA Ops:
  0.0 2.2 %shard_map.28 = (bf16[128,768]{1,0:T(8,128)(2,1)S(1)}, bf16[128,768]{1,0:T(8,128)(2,1)S(1)}, s32[1,768]{1,0:T(1,128)S(1)}, f32[8,128]{1,0:T(8,128)S(1)}, bf16[768,768]{1,0:T(8,128)(2,1)S(1)}) custom-call(s32[768]{0:T(1024)} %cluster_ref.1, f32[768,768]{1,0:T(8,128)} %rows_ref.1), custom_call_target="tpu_custom_call" | custom-call | flops 301989888 | bytes 2752512 | tf_op jit(solution)/shard_map/pallas_call | solution.py:107
  2.2 4.1 %collective-permute-start = (bf16[128,768]{1,0:T(8,128)(2,1)S(1)}, bf16[128,768]{1,0:T(8,128)(2,1)S(1)}, u32[]{:S(2)}, u32[]{:S(2)}) collective-permute-start(bf16[128,768]{1,0:T(8,128)(2,1)S(1)} %get-tuple-element.22), channel_id=1, source_target_pairs={{0,8},{1,9},{2,10},{3,11},{4,12},{5,13},{6,14},{7,15},{8,0},{9,1},... | collective-permute-start | bytes 589832 | tf_op jit(solution)/shard_map/ppermute | solution.py:268
  6.3 1.3 %collective-permute-start.1 = (bf16[128,768]{1,0:T(8,128)(2,1)S(1)}, bf16[128,768]{1,0:T(8,128)(2,1)S(1)}, u32[]{:S(2)}, u32[]{:S(2)}) collective-permute-start(bf16[128,768]{1,0:T(8,128)(2,1)S(1)} %get-tuple-element.23), channel_id=1, source_target_pairs={{0,10},{1,11},{2,8},{3,9},{4,14},{5,15},{6,12},{7,13},{8,2},{9,3},... | collective-permute-start | bytes 589832 | tf_op jit(solution)/shard_map/ppermute | solution.py:268
  7.6 1.1 %shard_map.29 = (bf16[128,768]{1,0:T(8,128)(2,1)S(1)}, bf16[128,768]{1,0:T(8,128)(2,1)S(1)}, bf16[128,768]{1,0:T(8,128)(2,1)S(1)}, bf16[128,768]{1,0:T(8,128)(2,...) custom-call(s32[1,768]{1,0:T(1,128)S(1)} %get-tuple-element.18.slot_ref, ...), custom_call_target="tpu_custom_call" | custom-call | flops 905969664 | bytes 3538944 | tf_op jit(solution)/shard_map/pallas_call | solution.py:142
  8.7 0.3 collective-permute-start.2
  9.1 1.8 %collective-permute-start.3 = (bf16[128,768]{1,0:T(8,128)(2,1)S(1)}, bf16[128,768]{1,0:T(8,128)(2,1)S(1)}, u32[]{:S(2)}, u32[]{:S(2)}) collective-permute-start(bf16[128,768]{1,0:T(8,128)(2,1)S(1)} %get-tuple-element.25), channel_id=1, source_target_pairs={{0,4},{1,5},{2,6},{3,7},{4,0},{5,1},{6,2},{7,3},{8,12},{9,13},{10,... | collective-permute-start | bytes 589832 | tf_op jit(solution)/shard_map/ppermute | solution.py:268
  10.9 1.4 %collective-permute-start.4 = (bf16[128,768]{1,0:T(8,128)(2,1)S(1)}, bf16[128,768]{1,0:T(8,128)(2,1)S(1)}, u32[]{:S(2)}, u32[]{:S(2)}) collective-permute-start(bf16[128,768]{1,0:T(8,128)(2,1)S(1)} %get-tuple-element.26), channel_id=1, source_target_pairs={{0,6},{1,7},{2,4},{3,5},{4,2},{5,3},{6,0},{7,1},{8,14},{9,15},{10,... | collective-permute-start | bytes 589832 | tf_op jit(solution)/shard_map/ppermute | solution.py:268
  12.3 8.3 %collective-permute-done = bf16[128,768]{1,0:T(8,128)(2,1)S(1)} collective-permute-done((bf16[128,768]{1,0:T(8,128)(2,1)S(1)}, bf16[128,768]{1,0:T(8,128)(2,1)S(1)}, u32[]{:S(2)}, u32[]{:S(2)}) %collective-permute-start) | collective-permute-done | bytes 196640 | tf_op jit(solution)/shard_map/ppermute | solution.py:268
  20.6 2.8 %collective-permute-start.5 = (bf16[128,768]{1,0:T(8,128)(2,1)S(1)}, bf16[128,768]{1,0:T(8,128)(2,1)S(1)}, u32[]{:S(2)}, u32[]{:S(2)}) collective-permute-start(bf16[128,768]{1,0:T(8,128)(2,1)S(1)} %get-tuple-element.28), channel_id=1, source_target_pairs={{0,12},{1,13},{2,14},{3,15},{4,8},{5,9},{6,10},{7,11},{8,4},{9,5},... | collective-permute-start | bytes 589832 | tf_op jit(solution)/shard_map/ppermute | solution.py:268
  23.4 3.5 %collective-permute-done.1 = bf16[128,768]{1,0:T(8,128)(2,1)S(1)} collective-permute-done((bf16[128,768]{1,0:T(8,128)(2,1)S(1)}, bf16[128,768]{1,0:T(8,128)(2,1)S(1)}, u32[]{:S(2)}, u32[]{:S(2)}) %collective-permute-start.1) | collective-permute-done | bytes 196640 | tf_op jit(solution)/shard_map/ppermute | solution.py:268
  26.9 1.5 %collective-permute-start.6 = (bf16[128,768]{1,0:T(8,128)(2,1)S(1)}, bf16[128,768]{1,0:T(8,128)(2,1)S(1)}, u32[]{:S(2)}, u32[]{:S(2)}) collective-permute-start(bf16[128,768]{1,0:T(8,128)(2,1)S(1)} %get-tuple-element.30), channel_id=1, source_target_pairs={{0,14},{1,15},{2,12},{3,13},{4,10},{5,11},{6,8},{7,9},{8,6},{9,7},... | collective-permute-start | bytes 589832 | tf_op jit(solution)/shard_map/ppermute | solution.py:268
  28.5 0.0 collective-permute-done.2
  28.5 0.1 collective-permute-start.7
  28.6 0.0 collective-permute-done.3
  28.6 7.4 %collective-permute-done.4 = bf16[128,768]{1,0:T(8,128)(2,1)S(1)} collective-permute-done((bf16[128,768]{1,0:T(8,128)(2,1)S(1)}, bf16[128,768]{1,0:T(8,128)(2,1)S(1)}, u32[]{:S(2)}, u32[]{:S(2)}) %collective-permute-start.4) | collective-permute-done | bytes 196640 | tf_op jit(solution)/shard_map/ppermute | solution.py:268
  36.1 0.0 collective-permute-done.5
  36.1 0.0 collective-permute-done.6
  36.1 0.1 collective-permute-start.8
  36.2 0.0 collective-permute-done.7.refs_1_.refs_2_
  36.2 1.1 %shard_map.30.refs_2_ = f32[4,128]{1,0:T(4,128)S(1)} custom-call(bf16[512,768]{1,0:T(8,128)(2,1)S(1)} %constant_dynamic-update-slice_fusion.refs_0_, bf16[512,768]{1,0:T(8,128)(2,1)S(1)} %collective-permute-done.7.refs_1_.refs_2_), custom_call_target="tpu_custom_call" | custom-call | flops 805306368 | bytes 1572864 | tf_op jit(solution)/shard_map/pallas_call | solution.py:222
  37.3 1.5 %shard_map.31.refs_4_ = f32[8,128]{1,0:T(8,128)S(1)} custom-call(bf16[512,768]{1,0:T(8,128)(2,1)S(1)} %constant_dynamic-update-slice_fusion.refs_0_, bf16[512,768]{1,0:T(8,128)(2,1)S(1)} %constant_dynamic-update-slice_fusion.4.refs_1_, f32[4,128]{1,0:T(4,128)S(1)} %shard_map.30.refs_2_), custom_call_target="tpu_custom_call" | custom-call | flops 1207959552 | bytes 1572864 | tf_op jit(solution)/shard_map/pallas_call | solution.py:222
  38.7 0.0 collective-permute-done.8.refs_3_
  38.7 1.4 %shard_map.32 = f32[8,128]{1,0:T(8,128)S(1)} custom-call(bf16[512,768]{1,0:T(8,128)(2,1)S(1)} %constant_dynamic-update-slice_fusion.refs_0_, bf16[512,768]{1,0:T(8,128)(2,1)S(1)} %constant_dynamic-update-slice_fusion.4.refs_1_, bf16[512,768]{1,0:T(8,128)(2,1)S(1)} %collective-permute-done.7.refs_1_.refs_2_, ...), custom_call_target="tpu_custom_call" | custom-call | flops 1207959552 | bytes 3145728 | tf_op jit(solution)/shard_map/pallas_call | solution.py:222
  40.2 15.8 %all_to_all.11 = f32[8,1,128]{2,1,0:T(1,128)S(1)} all-to-all(f32[8,1,128]{2,1,0:T(1,128)S(1)} %bitcast.5), channel_id=1, replica_groups={{0,2,4,6,8,10,12,14},{1,3,5,7,9,11,13,15},{16,18,20,22,24,26,28,30},{17..., dimensions={0} | all-to-all | bytes 8192 | tf_op jit(solution)/shard_map/all_to_all | solution.py:311
  56.0 0.8 %shard_map.33 = f32[768]{0:T(1024)} custom-call(s32[1,768]{1,0:T(1,128)S(1)} %get-tuple-element.18.slot_ref, f32[8,128]{1,0:T(8,128)S(1)} %bitcast.4), custom_call_target="tpu_custom_call" | custom-call | tf_op jit(solution)/shard_map/pallas_call | solution.py:258
  (8 shorter events, 0.1 us)
Async XLA Ops:
  2.2 18.4 %collective-permute-start = (bf16[128,768]{1,0:T(8,128)(2,1)S(1)}, bf16[128,768]{1,0:T(8,128)(2,1)S(1)}, u32[]{:S(2)}, u32[]{:S(2)}) collective-permute-start(bf16[128,768]{1,0:T(8,128)(2,1)S(1)} %get-tuple-element.22), channel_id=1, source_target_pairs={{0,8},{1,9},{2,10},{3,11},{4,12},{5,13},{6,14},{7,15},{8,0},{9,1},... | collective-permute-start | bytes 589832 | tf_op jit(solution)/shard_map/ppermute | solution.py:268
  6.3 20.6 %collective-permute-start.1 = (bf16[128,768]{1,0:T(8,128)(2,1)S(1)}, bf16[128,768]{1,0:T(8,128)(2,1)S(1)}, u32[]{:S(2)}, u32[]{:S(2)}) collective-permute-start(bf16[128,768]{1,0:T(8,128)(2,1)S(1)} %get-tuple-element.23), channel_id=1, source_target_pairs={{0,10},{1,11},{2,8},{3,9},{4,14},{5,15},{6,12},{7,13},{8,2},{9,3},... | collective-permute-start | bytes 589832 | tf_op jit(solution)/shard_map/ppermute | solution.py:268
  8.7 19.7 %collective-permute-start.2 = (bf16[128,768]{1,0:T(8,128)(2,1)S(1)}, bf16[128,768]{1,0:T(8,128)(2,1)S(1)}, u32[]{:S(2)}, u32[]{:S(2)}) collective-permute-start(bf16[128,768]{1,0:T(8,128)(2,1)S(1)} %get-tuple-element.24), channel_id=1, source_target_pairs={{0,2},{1,3},{2,0},{3,1},{4,6},{5,7},{6,4},{7,5},{8,10},{9,11},{10,... | collective-permute-start | bytes 589832 | tf_op jit(solution)/shard_map/ppermute | solution.py:268
  9.1 19.5 %collective-permute-start.3 = (bf16[128,768]{1,0:T(8,128)(2,1)S(1)}, bf16[128,768]{1,0:T(8,128)(2,1)S(1)}, u32[]{:S(2)}, u32[]{:S(2)}) collective-permute-start(bf16[128,768]{1,0:T(8,128)(2,1)S(1)} %get-tuple-element.25), channel_id=1, source_target_pairs={{0,4},{1,5},{2,6},{3,7},{4,0},{5,1},{6,2},{7,3},{8,12},{9,13},{10,... | collective-permute-start | bytes 589832 | tf_op jit(solution)/shard_map/ppermute | solution.py:268
  10.9 25.1 %collective-permute-start.4 = (bf16[128,768]{1,0:T(8,128)(2,1)S(1)}, bf16[128,768]{1,0:T(8,128)(2,1)S(1)}, u32[]{:S(2)}, u32[]{:S(2)}) collective-permute-start(bf16[128,768]{1,0:T(8,128)(2,1)S(1)} %get-tuple-element.26), channel_id=1, source_target_pairs={{0,6},{1,7},{2,4},{3,5},{4,2},{5,3},{6,0},{7,1},{8,14},{9,15},{10,... | collective-permute-start | bytes 589832 | tf_op jit(solution)/shard_map/ppermute | solution.py:268
  20.6 15.5 %collective-permute-start.5 = (bf16[128,768]{1,0:T(8,128)(2,1)S(1)}, bf16[128,768]{1,0:T(8,128)(2,1)S(1)}, u32[]{:S(2)}, u32[]{:S(2)}) collective-permute-start(bf16[128,768]{1,0:T(8,128)(2,1)S(1)} %get-tuple-element.28), channel_id=1, source_target_pairs={{0,12},{1,13},{2,14},{3,15},{4,8},{5,9},{6,10},{7,11},{8,4},{9,5},... | collective-permute-start | bytes 589832 | tf_op jit(solution)/shard_map/ppermute | solution.py:268
  26.9 9.2 %collective-permute-start.6 = (bf16[128,768]{1,0:T(8,128)(2,1)S(1)}, bf16[128,768]{1,0:T(8,128)(2,1)S(1)}, u32[]{:S(2)}, u32[]{:S(2)}) collective-permute-start(bf16[128,768]{1,0:T(8,128)(2,1)S(1)} %get-tuple-element.30), channel_id=1, source_target_pairs={{0,14},{1,15},{2,12},{3,13},{4,10},{5,11},{6,8},{7,9},{8,6},{9,7},... | collective-permute-start | bytes 589832 | tf_op jit(solution)/shard_map/ppermute | solution.py:268
  28.5 7.7 %collective-permute-start.7 = (bf16[512,768]{1,0:T(8,128)(2,1)S(1)}, bf16[512,768]{1,0:T(8,128)(2,1)S(1)}, u32[]{:S(2)}, u32[]{:S(2)}) collective-permute-start(bf16[512,768]{1,0:T(8,128)(2,1)S(1)} %constant_dynamic-update-slice_fusion.refs_0_), channel_id=1, source_target_pairs={{0,1},{1,0},{2,3},{3,2},{4,5},{5,4},{6,7},{7,6},{8,9},{9,8},{10,11... | collective-permute-start | bytes 2359304 | tf_op jit(solution)/shard_map/ppermute | solution.py:268
  36.1 2.6 %collective-permute-start.8 = (bf16[512,768]{1,0:T(8,128)(2,1)S(1)}, bf16[512,768]{1,0:T(8,128)(2,1)S(1)}, u32[]{:S(2)}, u32[]{:S(2)}) collective-permute-start(bf16[512,768]{1,0:T(8,128)(2,1)S(1)} %constant_dynamic-update-slice_fusion.4.refs_1_), channel_id=1, source_target_pairs={{0,1},{1,0},{2,3},{3,2},{4,5},{5,4},{6,7},{7,6},{8,9},{9,8},{10,11... | collective-permute-start | bytes 2359304 | tf_op jit(solution)/shard_map/ppermute | solution.py:268

commit v4 on v3

--- a/solution.py
+++ b/solution.py
@@ -190,9 +190,9 @@
     best_ref = refs[-1]
     chip = lax.axis_index("owners") // 2 if order else 0
     at = 0
-    for query_block, key_blocks, starts in plan:
+    for query_blocks, key_blocks, starts in plan:
         first = 0
-        for query_group in pieces([refs[query_block]], 256):
+        for query_group in pieces([refs[block] for block in query_blocks], 256):
             query = load(query_group)
             wide = query.shape[0]
             best = jnp.full((8, wide), FLOOR, jnp.float32)
@@ -200,7 +200,7 @@
                 key_first = 0
                 for key_group in pieces([refs[key_block]], 512):
                     key = load(key_group)
-                    shift = first - key_first if key_block == query_block else None
+                    shift = first - key_first if (key_block,) == query_blocks else None
                     best = jnp.maximum(best, tile_best(key, query, shift))
                     key_first += key.shape[0]
             row = jnp.max(best, axis=0, keepdims=True)
@@ -215,8 +215,10 @@
 
 
 def score(blocks, plan, start=None, order=None):
-    n_query = sum(blocks[query].shape[0] for query, _, _ in plan)
-    pairs = sum(blocks[query].shape[0] * blocks[key].shape[0] for query, keys, _ in plan for key in keys)
+    n_query = sum(blocks[query].shape[0] for queries, _, _ in plan for query in queries)
+    pairs = sum(
+        blocks[query].shape[0] * blocks[key].shape[0] for queries, keys, _ in plan for query in queries for key in keys
+    )
     width = blocks[0].shape[1]
     args = [*blocks] + ([] if start is None else [start])
     return pl.pallas_call(
@@ -286,18 +288,23 @@
         got, packed = pack(cluster_of, embeddings, [(index, 1) for index in first], clusters, capacity, mixed)
         blocks.update(zip(first, got))
         blocks.update(zip(then, pack_more(packed, [(index, 1) for index in then], capacity)))
-        waits = {6: (4,), 7: (5,)}
         have = {0: blocks[0]}
-        for index in (4, 5, 1, 2, 3, 6, 7):
-            have[index] = send(after(blocks[index], *[have[wait] for wait in waits.get(index, ())]), index)
-        early = jnp.concatenate([have[index] for index in [0, 4, 5, 1]], axis=0)
+        for index in (4, 5, 1, 2, 3):
+            have[index] = send(blocks[index], index)
+        have[6] = send(after(blocks[6], have[4]), 6)
+        join = lambda *group: jnp.concatenate([have[index] for index in group], axis=0)
+        early = join(0, 4, 5, 1)
+        best = score([early], [((0,), [0], False)])
+        have[7] = send(after(blocks[7], best), 7)
         early_other = swap(early)
-        best = score([early, early_other], [(0, [0, 1], False)])
-        late = jnp.concatenate([have[index] for index in [2, 3, 6, 7]], axis=0)
-        late_other = swap(late)
-        best = score([early, late], [(0, [1], True), (1, [0, 1], False)], best)
+        mid = join(2, 3, 6)
+        best = score([early, mid], [((0,), [1], True), ((1,), [0, 1], False)], best)
+        late = have[7] = after(have[7], best)
+        near_other, late_other = swap(join(2, 3)), swap(join(6, 7))
+        best = score([early, mid, late], [((0, 1), [2], True), ((2,), [0, 1, 2], False)], best)
+        best = score([early, mid, late, early_other, near_other], [((0, 1, 2), [3, 4], True)], best)
         best = score(
-            [early, late, early_other, late_other], [(0, [3], True), (1, [2, 3], True)], best, [0, 4, 5, 1, 2, 3, 6, 7]
+            [early, mid, late, late_other], [((0, 1, 2), [3], True)], best, [0, 4, 5, 1, 2, 3, 6, 7]
         )
         slots = packed[0]
     else:
@@ -306,8 +313,8 @@
             outgoing.reshape(clusters, capacity, -1), "owners", 0, 0, axis_index_groups=same_core, tiled=True
         ).reshape(SLOTS, -1)
         other = by_xor(own, "owners", 1)
-        best = score([own], [(0, [0], False)])
-        best = score([own, other], [(0, [1], True)], best).reshape(clusters, capacity)
+        best = score([own], [((0,), [0], False)])
+        best = score([own, other], [((0,), [1], True)], best).reshape(clusters, capacity)
     answers = lax.all_to_all(best, "owners", 0, 0, axis_index_groups=same_core, tiled=True)
     return lookup(slots, answers, capacity, mixed)
 

time: 57 us -> 56.2 us (0.986)
  blocking collectives: 15.8 us -> 10.5 us
  waiting for transfers between devices: 19.2 us -> 21 us
  starting transfers between devices: 13.4 us -> 15 us
  Pallas kernels: 8.07 us -> 9.14 us
    all_to_all x1, blocking collectives: 15.8 us -> 10.5 us  [on_device(): lax.all_to_all(best, 'owners', 0, 0, axis_index_groups=same_core, tiled=T...]
    ppermute x9 -> x10, waiting for transfers between devices: 19.2 us -> 21 us  [by_xor(): lax.ppermute(value, axis, [(source, source ^ mask) for source in range(la...]
    ppermute x9 -> x10, starting transfers between devices: 13.4 us -> 15 us  [by_xor(): lax.ppermute(value, axis, [(source, source ^ mask) for source in range(la...]
    pallas_call x3 -> x5, Pallas kernels: 3.95 us -> 5.02 us  [score(): pl.pallas_call(functools.partial(score_kernel, plan, len(blocks), start i...]
  transfers between devices with their start and end apart: 9 -> 10, of which waited for: 3 -> 3; matrix products, arithmetic and copies ran while one was open for 0% -> 0% of each run, Pallas kernels for 6% -> 10%
where the time goes in v4:
time: 56.2 us; the launch traced here: 56 us
  waiting for transfers between devices  21 us (37%)
  starting transfers between devices  15 us (27%)
  blocking collectives  10.5 us (19%)
  Pallas kernels  9.14 us (16%)
    ppermute x10, waiting for transfers between devices, by_xor(): lax.ppermute(value, axis, [(source, source ^ mask) for source in range(la...  21 us
    ppermute x10, starting transfers between devices, by_xor(): lax.ppermute(value, axis, [(source, source ^ mask) for source in range(la...  15 us
    all_to_all x1, blocking collectives, on_device(): lax.all_to_all(best, 'owners', 0, 0, axis_index_groups=same_core, tiled=T...  10.5 us
    pallas_call x5, Pallas kernels, score(): pl.pallas_call(functools.partial(score_kernel, plan, len(blocks), start i...  5.02 us
    pallas_call x1, Pallas kernels, pack(): pl.pallas_call(functools.partial(pack_kernel, taken, mixed, clusters, cap...  2.21 us
  transfers between devices with their start and end apart: 10, of which 3 were waited for; matrix products, arithmetic and copies ran while one was open for 0% of the time, Pallas kernels for 10%

profile of v4, /device:TPU:0, one launch (start us, length us, event | category | flops | bytes accessed | tf_op | source)
XLA Modules:
  0.0 56.0 jit_solution(9812356714878284854)
XLA Ops:
  0.0 2.2 %shard_map.28 = (bf16[128,768]{1,0:T(8,128)(2,1)S(1)}, bf16[128,768]{1,0:T(8,128)(2,1)S(1)}, s32[1,768]{1,0:T(1,128)S(1)}, f32[8,128]{1,0:T(8,128)S(1)}, bf16[768,768]{1,0:T(8,128)(2,1)S(1)}) custom-call(s32[768]{0:T(1024)} %cluster_ref.1, f32[768,768]{1,0:T(8,128)} %rows_ref.1), custom_call_target="tpu_custom_call" | custom-call | flops 301989888 | bytes 2752512 | tf_op jit(solution)/shard_map/pallas_call | solution.py:107
  2.2 4.1 %collective-permute-start = (bf16[128,768]{1,0:T(8,128)(2,1)S(1)}, bf16[128,768]{1,0:T(8,128)(2,1)S(1)}, u32[]{:S(2)}, u32[]{:S(2)}) collective-permute-start(bf16[128,768]{1,0:T(8,128)(2,1)S(1)} %get-tuple-element.23), channel_id=1, source_target_pairs={{0,8},{1,9},{2,10},{3,11},{4,12},{5,13},{6,14},{7,15},{8,0},{9,1},... | collective-permute-start | bytes 589832 | tf_op jit(solution)/shard_map/ppermute | solution.py:270
  6.3 1.1 %shard_map.29 = (bf16[128,768]{1,0:T(8,128)(2,1)S(1)}, bf16[128,768]{1,0:T(8,128)(2,1)S(1)}, bf16[128,768]{1,0:T(8,128)(2,1)S(1)}, bf16[128,768]{1,0:T(8,128)(2,...) custom-call(s32[1,768]{1,0:T(1,128)S(1)} %get-tuple-element.19.slot_ref, ...), custom_call_target="tpu_custom_call" | custom-call | flops 905969664 | bytes 3538944 | tf_op jit(solution)/shard_map/pallas_call | solution.py:142
  7.4 1.6 %collective-permute-start.2 = (bf16[128,768]{1,0:T(8,128)(2,1)S(1)}, bf16[128,768]{1,0:T(8,128)(2,1)S(1)}, u32[]{:S(2)}, u32[]{:S(2)}) collective-permute-start(bf16[128,768]{1,0:T(8,128)(2,1)S(1)} %get-tuple-element.25), channel_id=1, source_target_pairs={{0,2},{1,3},{2,0},{3,1},{4,6},{5,7},{6,4},{7,5},{8,10},{9,11},{10,... | collective-permute-start | bytes 589832 | tf_op jit(solution)/shard_map/ppermute | solution.py:270
  9.0 1.6 %collective-permute-start.3 = (bf16[128,768]{1,0:T(8,128)(2,1)S(1)}, bf16[128,768]{1,0:T(8,128)(2,1)S(1)}, u32[]{:S(2)}, u32[]{:S(2)}) collective-permute-start(bf16[128,768]{1,0:T(8,128)(2,1)S(1)} %get-tuple-element.26), channel_id=1, source_target_pairs={{0,4},{1,5},{2,6},{3,7},{4,0},{5,1},{6,2},{7,3},{8,12},{9,13},{10,... | collective-permute-start | bytes 589832 | tf_op jit(solution)/shard_map/ppermute | solution.py:270
  10.6 0.4 collective-permute-start.4
  11.0 1.3 %collective-permute-start.1 = (bf16[128,768]{1,0:T(8,128)(2,1)S(1)}, bf16[128,768]{1,0:T(8,128)(2,1)S(1)}, u32[]{:S(2)}, u32[]{:S(2)}) collective-permute-start(bf16[128,768]{1,0:T(8,128)(2,1)S(1)} %get-tuple-element.24), channel_id=1, source_target_pairs={{0,10},{1,11},{2,8},{3,9},{4,14},{5,15},{6,12},{7,13},{8,2},{9,3},... | collective-permute-start | bytes 589832 | tf_op jit(solution)/shard_map/ppermute | solution.py:270
  12.3 4.1 %collective-permute-done = bf16[128,768]{1,0:T(8,128)(2,1)S(1)} collective-permute-done((bf16[128,768]{1,0:T(8,128)(2,1)S(1)}, bf16[128,768]{1,0:T(8,128)(2,1)S(1)}, u32[]{:S(2)}, u32[]{:S(2)}) %collective-permute-start) | collective-permute-done | bytes 196640 | tf_op jit(solution)/shard_map/ppermute | solution.py:270
  16.4 2.8 %collective-permute-start.5 = (bf16[128,768]{1,0:T(8,128)(2,1)S(1)}, bf16[128,768]{1,0:T(8,128)(2,1)S(1)}, u32[]{:S(2)}, u32[]{:S(2)}) collective-permute-start(bf16[128,768]{1,0:T(8,128)(2,1)S(1)} %get-tuple-element.29), channel_id=1, source_target_pairs={{0,12},{1,13},{2,14},{3,15},{4,8},{5,9},{6,10},{7,11},{8,4},{9,5},... | collective-permute-start | bytes 589832 | tf_op jit(solution)/shard_map/ppermute | solution.py:270
  19.2 11.2 %collective-permute-done.1 = bf16[128,768]{1,0:T(8,128)(2,1)S(1)} collective-permute-done((bf16[128,768]{1,0:T(8,128)(2,1)S(1)}, bf16[128,768]{1,0:T(8,128)(2,1)S(1)}, u32[]{:S(2)}, u32[]{:S(2)}) %collective-permute-start.1) | collective-permute-done | bytes 196640 | tf_op jit(solution)/shard_map/ppermute | solution.py:270
  30.4 0.0 collective-permute-done.2
  30.4 0.1 collective-permute-start.8
  30.5 0.6 %shard_map.30.refs_2_ = f32[4,128]{1,0:T(4,128)S(1)} custom-call(bf16[512,768]{1,0:T(8,128)(2,1)S(1)} %constant_dynamic-update-slice_fusion.refs_0_), custom_call_target="tpu_custom_call" | custom-call | flops 402653184 | bytes 786432 | tf_op jit(solution)/shard_map/pallas_call | solution.py:224
  31.1 0.0 collective-permute-done.3
  31.1 0.0 collective-permute-done.4
  31.1 0.6 %collective-permute-start.9 = (bf16[256,768]{1,0:T(8,128)(2,1)S(1)}, bf16[256,768]{1,0:T(8,128)(2,1)S(1)}, u32[]{:S(2)}, u32[]{:S(2)}) collective-permute-start(bf16[256,768]{1,0:T(8,128)(2,1)S(1)} %pad_maximum_fusion.1), channel_id=1, source_target_pairs={{0,1},{1,0},{2,3},{3,2},{4,5},{5,4},{6,7},{7,6},{8,9},{9,8},{10,11... | collective-permute-start | bytes 1179656 | tf_op jit(solution)/shard_map/ppermute | solution.py:270
  31.7 2.6 %collective-permute-start.6 = (bf16[128,768]{1,0:T(8,128)(2,1)S(1)}, bf16[128,768]{1,0:T(8,128)(2,1)S(1)}, u32[]{:S(2)}, u32[]{:S(2)}) collective-permute-start(bf16[128,768]{1,0:T(8,128)(2,1)S(1)} %get-tuple-element.31), channel_id=1, source_target_pairs={{0,14},{1,15},{2,12},{3,13},{4,10},{5,11},{6,8},{7,9},{8,6},{9,7},... | collective-permute-start | bytes 589832 | tf_op jit(solution)/shard_map/ppermute | solution.py:270
  34.3 0.0 collective-permute-done.5
  34.4 1.3 %shard_map.31.refs_3_ = f32[7,128]{1,0:T(8,128)S(1)} custom-call(bf16[512,768]{1,0:T(8,128)(2,1)S(1)} %constant_dynamic-update-slice_fusion.refs_0_, bf16[384,768]{1,0:T(8,128)(2,1)S(1)} %constant_dynamic-update-slice_fusion.4.refs_1_, f32[4,128]{1,0:T(4,128)S(1)} %shard_map.30.refs_2_), custom_call_target="tpu_custom_call" | custom-call | flops 830472192 | bytes 1376256 | tf_op jit(solution)/shard_map/pallas_call | solution.py:224
  35.6 5.8 %collective-permute-done.6.refs_2_ = bf16[128,768]{1,0:T(8,128)(2,1)S(1)} collective-permute-done((bf16[128,768]{1,0:T(8,128)(2,1)S(1)}, bf16[128,768]{1,0:T(8,128)(2,1)S(1)}, u32[]{:S(2)}, u32[]{:S(2)}) %collective-permute-start.6) | collective-permute-done | bytes 196640 | tf_op jit(solution)/shard_map/ppermute | solution.py:270
  41.4 0.1 collective-permute-start.7
  41.5 1.0 %shard_map.32.refs_5_ = f32[8,128]{1,0:T(8,128)S(1)} custom-call(bf16[512,768]{1,0:T(8,128)(2,1)S(1)} %constant_dynamic-update-slice_fusion.refs_0_, bf16[384,768]{1,0:T(8,128)(2,1)S(1)} %constant_dynamic-update-slice_fusion.4.refs_1_, bf16[128,768]{1,0:T(8,128)(2,1)S(1)} %collective-permute-done.6.refs_2_, f32[7,128]{1,0:T(8,128)S(1)} %shard_map.31.refs_3_), custom_call_target="tpu_custom_call" | custom-call | flops 377487360 | bytes 1572864 | tf_op jit(solution)/shard_map/pallas_call | solution.py:224
  42.5 0.0 collective-permute-done.9.refs_4_
  42.5 0.0 collective-permute-done.8.refs_3_
  42.5 1.5 %shard_map.33.refs_4_ = f32[8,128]{1,0:T(8,128)S(1)} custom-call(bf16[512,768]{1,0:T(8,128)(2,1)S(1)} %constant_dynamic-update-slice_fusion.refs_0_, bf16[384,768]{1,0:T(8,128)(2,1)S(1)} %constant_dynamic-update-slice_fusion.4.refs_1_, bf16[128,768]{1,0:T(8,128)(2,1)S(1)} %collective-permute-done.6.refs_2_, ...), custom_call_target="tpu_custom_call" | custom-call | flops 1207959552 | bytes 2752512 | tf_op jit(solution)/shard_map/pallas_call | solution.py:224
  44.1 0.0 collective-permute-done.7.refs_3_
  44.1 0.6 %shard_map.34 = f32[8,128]{1,0:T(8,128)S(1)} custom-call(bf16[512,768]{1,0:T(8,128)(2,1)S(1)} %constant_dynamic-update-slice_fusion.refs_0_, bf16[384,768]{1,0:T(8,128)(2,1)S(1)} %constant_dynamic-update-slice_fusion.4.refs_1_, bf16[128,768]{1,0:T(8,128)(2,1)S(1)} %collective-permute-done.6.refs_2_, bf16[256,768]{1,0:T(8,128)(2,1)S(1)} %collective-permute-done.7.refs_3_, ...), custom_call_target="tpu_custom_call" | custom-call | flops 402653184 | bytes 1966080 | tf_op jit(solution)/shard_map/pallas_call | solution.py:224
  44.7 10.5 %all_to_all.11 = f32[8,1,128]{2,1,0:T(1,128)S(1)} all-to-all(f32[8,1,128]{2,1,0:T(1,128)S(1)} %bitcast.4), channel_id=1, replica_groups={{0,2,4,6,8,10,12,14},{1,3,5,7,9,11,13,15},{16,18,20,22,24,26,28,30},{17..., dimensions={0} | all-to-all | bytes 8192 | tf_op jit(solution)/shard_map/all_to_all | solution.py:318
  55.2 0.8 %shard_map.35 = f32[768]{0:T(1024)} custom-call(s32[1,768]{1,0:T(1,128)S(1)} %get-tuple-element.19.slot_ref, f32[8,128]{1,0:T(8,128)S(1)} %bitcast.5), custom_call_target="tpu_custom_call" | custom-call | tf_op jit(solution)/shard_map/pallas_call | solution.py:260
  (9 shorter events, 0.2 us)
Async XLA Ops:
  2.2 14.1 %collective-permute-start = (bf16[128,768]{1,0:T(8,128)(2,1)S(1)}, bf16[128,768]{1,0:T(8,128)(2,1)S(1)}, u32[]{:S(2)}, u32[]{:S(2)}) collective-permute-start(bf16[128,768]{1,0:T(8,128)(2,1)S(1)} %get-tuple-element.23), channel_id=1, source_target_pairs={{0,8},{1,9},{2,10},{3,11},{4,12},{5,13},{6,14},{7,15},{8,0},{9,1},... | collective-permute-start | bytes 589832 | tf_op jit(solution)/shard_map/ppermute | solution.py:270
  7.4 22.9 %collective-permute-start.2 = (bf16[128,768]{1,0:T(8,128)(2,1)S(1)}, bf16[128,768]{1,0:T(8,128)(2,1)S(1)}, u32[]{:S(2)}, u32[]{:S(2)}) collective-permute-start(bf16[128,768]{1,0:T(8,128)(2,1)S(1)} %get-tuple-element.25), channel_id=1, source_target_pairs={{0,2},{1,3},{2,0},{3,1},{4,6},{5,7},{6,4},{7,5},{8,10},{9,11},{10,... | collective-permute-start | bytes 589832 | tf_op jit(solution)/shard_map/ppermute | solution.py:270
  9.0 22.1 %collective-permute-start.3 = (bf16[128,768]{1,0:T(8,128)(2,1)S(1)}, bf16[128,768]{1,0:T(8,128)(2,1)S(1)}, u32[]{:S(2)}, u32[]{:S(2)}) collective-permute-start(bf16[128,768]{1,0:T(8,128)(2,1)S(1)} %get-tuple-element.26), channel_id=1, source_target_pairs={{0,4},{1,5},{2,6},{3,7},{4,0},{5,1},{6,2},{7,3},{8,12},{9,13},{10,... | collective-permute-start | bytes 589832 | tf_op jit(solution)/shard_map/ppermute | solution.py:270
  10.6 20.5 %collective-permute-start.4 = (bf16[128,768]{1,0:T(8,128)(2,1)S(1)}, bf16[128,768]{1,0:T(8,128)(2,1)S(1)}, u32[]{:S(2)}, u32[]{:S(2)}) collective-permute-start(bf16[128,768]{1,0:T(8,128)(2,1)S(1)} %get-tuple-element.27), channel_id=1, source_target_pairs={{0,6},{1,7},{2,4},{3,5},{4,2},{5,3},{6,0},{7,1},{8,14},{9,15},{10,... | collective-permute-start | bytes 589832 | tf_op jit(solution)/shard_map/ppermute | solution.py:270
  11.0 19.4 %collective-permute-start.1 = (bf16[128,768]{1,0:T(8,128)(2,1)S(1)}, bf16[128,768]{1,0:T(8,128)(2,1)S(1)}, u32[]{:S(2)}, u32[]{:S(2)}) collective-permute-start(bf16[128,768]{1,0:T(8,128)(2,1)S(1)} %get-tuple-element.24), channel_id=1, source_target_pairs={{0,10},{1,11},{2,8},{3,9},{4,14},{5,15},{6,12},{7,13},{8,2},{9,3},... | collective-permute-start | bytes 589832 | tf_op jit(solution)/shard_map/ppermute | solution.py:270
  16.4 18.0 %collective-permute-start.5 = (bf16[128,768]{1,0:T(8,128)(2,1)S(1)}, bf16[128,768]{1,0:T(8,128)(2,1)S(1)}, u32[]{:S(2)}, u32[]{:S(2)}) collective-permute-start(bf16[128,768]{1,0:T(8,128)(2,1)S(1)} %get-tuple-element.29), channel_id=1, source_target_pairs={{0,12},{1,13},{2,14},{3,15},{4,8},{5,9},{6,10},{7,11},{8,4},{9,5},... | collective-permute-start | bytes 589832 | tf_op jit(solution)/shard_map/ppermute | solution.py:270
  30.4 12.1 %collective-permute-start.8 = (bf16[512,768]{1,0:T(8,128)(2,1)S(1)}, bf16[512,768]{1,0:T(8,128)(2,1)S(1)}, u32[]{:S(2)}, u32[]{:S(2)}) collective-permute-start(bf16[512,768]{1,0:T(8,128)(2,1)S(1)} %constant_dynamic-update-slice_fusion.refs_0_), channel_id=1, source_target_pairs={{0,1},{1,0},{2,3},{3,2},{4,5},{5,4},{6,7},{7,6},{8,9},{9,8},{10,11... | collective-permute-start | bytes 2359304 | tf_op jit(solution)/shard_map/ppermute | solution.py:270
  31.1 11.4 %collective-permute-start.9 = (bf16[256,768]{1,0:T(8,128)(2,1)S(1)}, bf16[256,768]{1,0:T(8,128)(2,1)S(1)}, u32[]{:S(2)}, u32[]{:S(2)}) collective-permute-start(bf16[256,768]{1,0:T(8,128)(2,1)S(1)} %pad_maximum_fusion.1), channel_id=1, source_target_pairs={{0,1},{1,0},{2,3},{3,2},{4,5},{5,4},{6,7},{7,6},{8,9},{9,8},{10,11... | collective-permute-start | bytes 1179656 | tf_op jit(solution)/shard_map/ppermute | solution.py:270
  31.7 9.7 %collective-permute-start.6 = (bf16[128,768]{1,0:T(8,128)(2,1)S(1)}, bf16[128,768]{1,0:T(8,128)(2,1)S(1)}, u32[]{:S(2)}, u32[]{:S(2)}) collective-permute-start(bf16[128,768]{1,0:T(8,128)(2,1)S(1)} %get-tuple-element.31), channel_id=1, source_target_pairs={{0,14},{1,15},{2,12},{3,13},{4,10},{5,11},{6,8},{7,9},{8,6},{9,7},... | collective-permute-start | bytes 589832 | tf_op jit(solution)/shard_map/ppermute | solution.py:270
  41.4 2.6 %collective-permute-start.7 = (bf16[256,768]{1,0:T(8,128)(2,1)S(1)}, bf16[256,768]{1,0:T(8,128)(2,1)S(1)}, u32[]{:S(2)}, u32[]{:S(2)}) collective-permute-start(bf16[256,768]{1,0:T(8,128)(2,1)S(1)} %pad_maximum_fusion), channel_id=1, source_target_pairs={{0,1},{1,0},{2,3},{3,2},{4,5},{5,4},{6,7},{7,6},{8,9},{9,8},{10,11... | collective-permute-start | bytes 1179656 | tf_op jit(solution)/shard_map/ppermute | solution.py:270

commit v5 on v4

--- a/solution.py
+++ b/solution.py
@@ -172,15 +172,34 @@
     return parts[0] if len(parts) == 1 else jnp.concatenate(parts, axis=0)
 
 
-def tile_best(key, query, shift):
+def own_rows(shape, key_group, query_group):
+    found = None
+    key_at = 0
+    for key_ref, key_start, key_size in key_group:
+        query_at = 0
+        for query_ref, query_start, query_size in query_group:
+            if key_ref is query_ref and key_start < query_start + query_size and query_start < key_start + key_size:
+                row = lax.broadcasted_iota(jnp.int32, shape, 0)
+                lane = lax.broadcasted_iota(jnp.int32, shape, 1)
+                same = row - lane == query_start - query_at - key_start + key_at
+                if key_size < shape[0]:
+                    same = same & (row >= key_at) & (row < key_at + key_size)
+                if query_size < shape[1]:
+                    same = same & (lane >= query_at) & (lane < query_at + query_size)
+                found = same if found is None else found | same
+            query_at += query_size
+        key_at += key_size
+    return found
+
+
+def tile_best(key_group, query_group, query):
+    key = load(key_group)
     deep, wide = key.shape[0], query.shape[0]
     scores = lax.dot_general(key, query, (((1,), (1,)), ((), ())), preferred_element_type=jnp.float32)
     dead = key[:, :1].astype(jnp.float32) > 2.0
     scores = scores + jnp.where(dead, 2 * FLOOR, 0.0)
-    if shift is not None and -wide < shift < deep:
-        own = lax.broadcasted_iota(jnp.int32, scores.shape, 0) == (
-            lax.broadcasted_iota(jnp.int32, scores.shape, 1) + shift
-        )
+    own = own_rows(scores.shape, key_group, query_group)
+    if own is not None:
         scores = jnp.where(own, FLOOR, scores)
     return jnp.max(scores.reshape(deep // 8, 8, wide), axis=0)
 
@@ -189,29 +208,20 @@
     start_ref = refs[n_blocks] if has_start else None
     best_ref = refs[-1]
     chip = lax.axis_index("owners") // 2 if order else 0
-    at = 0
+    index = 0
     for query_blocks, key_blocks, starts in plan:
-        first = 0
         for query_group in pieces([refs[block] for block in query_blocks], 256):
             query = load(query_group)
-            wide = query.shape[0]
-            best = jnp.full((8, wide), FLOOR, jnp.float32)
-            for key_block in key_blocks:
-                key_first = 0
-                for key_group in pieces([refs[key_block]], 512):
-                    key = load(key_group)
-                    shift = first - key_first if (key_block,) == query_blocks else None
-                    best = jnp.maximum(best, tile_best(key, query, shift))
-                    key_first += key.shape[0]
+            best = jnp.full((8, query.shape[0]), FLOOR, jnp.float32)
+            for key_group in pieces([refs[block] for block in key_blocks], 512):
+                best = jnp.maximum(best, tile_best(key_group, query_group, query))
             row = jnp.max(best, axis=0, keepdims=True)
-            for lane in range(0, wide, LANES):
-                index = (at + first + lane) // LANES
+            for lane in range(0, query.shape[0], LANES):
                 part = row[:, lane : lane + LANES]
                 if starts:
                     part = jnp.maximum(part, start_ref[index : index + 1, :])
                 best_ref[pl.ds(lax.bitwise_xor(order[index], chip) if order else index, 1), :] = part
-            first += wide
-        at += first
+                index += 1
 
 
 def score(blocks, plan, start=None, order=None):
@@ -296,15 +306,20 @@
         early = join(0, 4, 5, 1)
         best = score([early], [((0,), [0], False)])
         have[7] = send(after(blocks[7], best), 7)
-        early_other = swap(early)
+        first_other, second_other = swap(join(0, 4)), swap(join(1, 5))
         mid = join(2, 3, 6)
+        near_other = swap(join(2, 3))
         best = score([early, mid], [((0,), [1], True), ((1,), [0, 1], False)], best)
+        best = score([early, mid, first_other, near_other], [((0, 1), [2, 3], True)], best)
         late = have[7] = after(have[7], best)
-        near_other, late_other = swap(join(2, 3)), swap(join(6, 7))
-        best = score([early, mid, late], [((0, 1), [2], True), ((2,), [0, 1, 2], False)], best)
-        best = score([early, mid, late, early_other, near_other], [((0, 1, 2), [3, 4], True)], best)
+        late_other = swap(join(6, 7))
         best = score(
-            [early, mid, late, late_other], [((0, 1, 2), [3], True)], best, [0, 4, 5, 1, 2, 3, 6, 7]
+            [early, mid, late, first_other, near_other, second_other],
+            [((0, 1), [5], True), ((2,), [0, 1, 3, 4, 5], False)],
+            best,
+        )
+        best = score(
+            [early, mid, late, late_other], [((0, 1, 2), [2, 3], True)], best, [0, 4, 5, 1, 2, 3, 6, 7]
         )
         slots = packed[0]
     else:

time: 56.2 us -> 55.5 us (0.988)
  blocking collectives: 10.5 us -> 14.8 us
  waiting for transfers between devices: 21 us -> 16.8 us
  starting transfers between devices: 15 us -> 14.1 us
    all_to_all x1, blocking collectives: 10.5 us -> 14.8 us  [on_device(): lax.all_to_all(best, 'owners', 0, 0, axis_index_groups=same_core, tiled=T...]
    ppermute x10 -> x11, waiting for transfers between devices: 21 us -> 16.8 us  [by_xor(): lax.ppermute(value, axis, [(source, source ^ mask) for source in range(la...]
    ppermute x10 -> x11, starting transfers between devices: 15 us -> 14.1 us  [by_xor(): lax.ppermute(value, axis, [(source, source ^ mask) for source in range(la...]
  transfers between devices with their start and end apart: 10 -> 11, of which waited for: 3 -> 4; matrix products, arithmetic and copies ran while one was open for 0% -> 0% of each run, Pallas kernels for 10% -> 10%
where the time goes in v5:
time: 55.5 us; the launch traced here: 55.3 us
  waiting for transfers between devices  16.8 us (30%)
  blocking collectives  14.8 us (27%)
  starting transfers between devices  14.1 us (25%)
  Pallas kernels  9.14 us (16%)
    ppermute x11, waiting for transfers between devices, by_xor(): lax.ppermute(value, axis, [(source, source ^ mask) for source in range(la...  16.8 us
    all_to_all x1, blocking collectives, on_device(): lax.all_to_all(best, 'owners', 0, 0, axis_index_groups=same_core, tiled=T...  14.8 us
    ppermute x11, starting transfers between devices, by_xor(): lax.ppermute(value, axis, [(source, source ^ mask) for source in range(la...  14.1 us
    pallas_call x5, Pallas kernels, score(): pl.pallas_call(functools.partial(score_kernel, plan, len(blocks), start i...  5.04 us
    pallas_call x1, Pallas kernels, pack(): pl.pallas_call(functools.partial(pack_kernel, taken, mixed, clusters, cap...  2.21 us
  transfers between devices with their start and end apart: 11, of which 4 were waited for; matrix products, arithmetic and copies ran while one was open for 0% of the time, Pallas kernels for 10%

profile of v5, /device:TPU:0, one launch (start us, length us, event | category | flops | bytes accessed | tf_op | source)
XLA Modules:
  0.0 55.3 jit_solution(5655239753802601709)
XLA Ops:
  0.0 2.2 %shard_map.28 = (bf16[128,768]{1,0:T(8,128)(2,1)S(1)}, bf16[128,768]{1,0:T(8,128)(2,1)S(1)}, s32[1,768]{1,0:T(1,128)S(1)}, f32[8,128]{1,0:T(8,128)S(1)}, bf16[768,768]{1,0:T(8,128)(2,1)S(1)}) custom-call(s32[768]{0:T(1024)} %cluster_ref.1, f32[768,768]{1,0:T(8,128)} %rows_ref.1), custom_call_target="tpu_custom_call" | custom-call | flops 301989888 | bytes 2752512 | tf_op jit(solution)/shard_map/pallas_call | solution.py:107
  2.2 4.1 %collective-permute-start = (bf16[128,768]{1,0:T(8,128)(2,1)S(1)}, bf16[128,768]{1,0:T(8,128)(2,1)S(1)}, u32[]{:S(2)}, u32[]{:S(2)}) collective-permute-start(bf16[128,768]{1,0:T(8,128)(2,1)S(1)} %get-tuple-element.23), channel_id=1, source_target_pairs={{0,8},{1,9},{2,10},{3,11},{4,12},{5,13},{6,14},{7,15},{8,0},{9,1},... | collective-permute-start | bytes 589832 | tf_op jit(solution)/shard_map/ppermute | solution.py:280
  6.3 1.3 %collective-permute-start.1 = (bf16[128,768]{1,0:T(8,128)(2,1)S(1)}, bf16[128,768]{1,0:T(8,128)(2,1)S(1)}, u32[]{:S(2)}, u32[]{:S(2)}) collective-permute-start(bf16[128,768]{1,0:T(8,128)(2,1)S(1)} %get-tuple-element.24), channel_id=1, source_target_pairs={{0,10},{1,11},{2,8},{3,9},{4,14},{5,15},{6,12},{7,13},{8,2},{9,3},... | collective-permute-start | bytes 589832 | tf_op jit(solution)/shard_map/ppermute | solution.py:280
  7.6 1.1 %shard_map.29 = (bf16[128,768]{1,0:T(8,128)(2,1)S(1)}, bf16[128,768]{1,0:T(8,128)(2,1)S(1)}, bf16[128,768]{1,0:T(8,128)(2,1)S(1)}, bf16[128,768]{1,0:T(8,128)(2,...) custom-call(s32[1,768]{1,0:T(1,128)S(1)} %get-tuple-element.19.slot_ref, ...), custom_call_target="tpu_custom_call" | custom-call | flops 905969664 | bytes 3538944 | tf_op jit(solution)/shard_map/pallas_call | solution.py:142
  8.7 0.3 collective-permute-start.2
  9.0 1.8 %collective-permute-start.3 = (bf16[128,768]{1,0:T(8,128)(2,1)S(1)}, bf16[128,768]{1,0:T(8,128)(2,1)S(1)}, u32[]{:S(2)}, u32[]{:S(2)}) collective-permute-start(bf16[128,768]{1,0:T(8,128)(2,1)S(1)} %get-tuple-element.26), channel_id=1, source_target_pairs={{0,4},{1,5},{2,6},{3,7},{4,0},{5,1},{6,2},{7,3},{8,12},{9,13},{10,... | collective-permute-start | bytes 589832 | tf_op jit(solution)/shard_map/ppermute | solution.py:280
  10.9 1.4 %collective-permute-start.4 = (bf16[128,768]{1,0:T(8,128)(2,1)S(1)}, bf16[128,768]{1,0:T(8,128)(2,1)S(1)}, u32[]{:S(2)}, u32[]{:S(2)}) collective-permute-start(bf16[128,768]{1,0:T(8,128)(2,1)S(1)} %get-tuple-element.27), channel_id=1, source_target_pairs={{0,6},{1,7},{2,4},{3,5},{4,2},{5,3},{6,0},{7,1},{8,14},{9,15},{10,... | collective-permute-start | bytes 589832 | tf_op jit(solution)/shard_map/ppermute | solution.py:280
  12.3 8.3 %collective-permute-done = bf16[128,768]{1,0:T(8,128)(2,1)S(1)} collective-permute-done((bf16[128,768]{1,0:T(8,128)(2,1)S(1)}, bf16[128,768]{1,0:T(8,128)(2,1)S(1)}, u32[]{:S(2)}, u32[]{:S(2)}) %collective-permute-start) | collective-permute-done | bytes 196640 | tf_op jit(solution)/shard_map/ppermute | solution.py:280
  20.6 2.8 %collective-permute-start.5 = (bf16[128,768]{1,0:T(8,128)(2,1)S(1)}, bf16[128,768]{1,0:T(8,128)(2,1)S(1)}, u32[]{:S(2)}, u32[]{:S(2)}) collective-permute-start(bf16[128,768]{1,0:T(8,128)(2,1)S(1)} %get-tuple-element.29), channel_id=1, source_target_pairs={{0,12},{1,13},{2,14},{3,15},{4,8},{5,9},{6,10},{7,11},{8,4},{9,5},... | collective-permute-start | bytes 589832 | tf_op jit(solution)/shard_map/ppermute | solution.py:280
  23.4 3.5 %collective-permute-done.1 = bf16[128,768]{1,0:T(8,128)(2,1)S(1)} collective-permute-done((bf16[128,768]{1,0:T(8,128)(2,1)S(1)}, bf16[128,768]{1,0:T(8,128)(2,1)S(1)}, u32[]{:S(2)}, u32[]{:S(2)}) %collective-permute-start.1) | collective-permute-done | bytes 196640 | tf_op jit(solution)/shard_map/ppermute | solution.py:280
  26.9 0.0 collective-permute-done.2
  26.9 0.6 %shard_map.30.refs_2_ = f32[4,128]{1,0:T(4,128)S(1)} custom-call(bf16[512,768]{1,0:T(8,128)(2,1)S(1)} %constant_dynamic-update-slice_fusion.refs_0_), custom_call_target="tpu_custom_call" | custom-call | flops 402653184 | bytes 786432 | tf_op jit(solution)/shard_map/pallas_call | solution.py:234
  27.6 1.6 %collective-permute-start.6 = (bf16[128,768]{1,0:T(8,128)(2,1)S(1)}, bf16[128,768]{1,0:T(8,128)(2,1)S(1)}, u32[]{:S(2)}, u32[]{:S(2)}) collective-permute-start(bf16[128,768]{1,0:T(8,128)(2,1)S(1)} %get-tuple-element.31), channel_id=1, source_target_pairs={{0,14},{1,15},{2,12},{3,13},{4,10},{5,11},{6,8},{7,9},{8,6},{9,7},... | collective-permute-start | bytes 589832 | tf_op jit(solution)/shard_map/ppermute | solution.py:280
  29.2 0.1 collective-permute-start.7
  29.3 0.0 collective-permute-done.3
  29.3 4.6 %collective-permute-done.4 = bf16[128,768]{1,0:T(8,128)(2,1)S(1)} collective-permute-done((bf16[128,768]{1,0:T(8,128)(2,1)S(1)}, bf16[128,768]{1,0:T(8,128)(2,1)S(1)}, u32[]{:S(2)}, u32[]{:S(2)}) %collective-permute-start.4) | collective-permute-done | bytes 196640 | tf_op jit(solution)/shard_map/ppermute | solution.py:280
  34.0 0.1 collective-permute-start.8
  34.1 0.6 %collective-permute-start.10 = (bf16[256,768]{1,0:T(8,128)(2,1)S(1)}, bf16[256,768]{1,0:T(8,128)(2,1)S(1)}, u32[]{:S(2)}, u32[]{:S(2)}) collective-permute-start(bf16[256,768]{1,0:T(8,128)(2,1)S(1)} %pad_maximum_fusion.3), channel_id=1, source_target_pairs={{0,1},{1,0},{2,3},{3,2},{4,5},{5,4},{6,7},{7,6},{8,9},{9,8},{10,11... | collective-permute-start | bytes 1179656 | tf_op jit(solution)/shard_map/ppermute | solution.py:280
  34.7 0.0 collective-permute-done.5
  34.7 1.3 %shard_map.31.refs_4_ = f32[7,128]{1,0:T(8,128)S(1)} custom-call(bf16[512,768]{1,0:T(8,128)(2,1)S(1)} %constant_dynamic-update-slice_fusion.refs_0_, bf16[384,768]{1,0:T(8,128)(2,1)S(1)} %constant_dynamic-update-slice_fusion.4.refs_1_, f32[4,128]{1,0:T(4,128)S(1)} %shard_map.30.refs_2_), custom_call_target="tpu_custom_call" | custom-call | flops 830472192 | bytes 1376256 | tf_op jit(solution)/shard_map/pallas_call | solution.py:234
  36.0 0.0 collective-permute-done.7.refs_2_.refs_3_
  36.0 0.0 collective-permute-done.8.refs_3_.refs_4_
  36.0 1.0 %shard_map.32.refs_6_ = f32[7,128]{1,0:T(8,128)S(1)} custom-call(bf16[512,768]{1,0:T(8,128)(2,1)S(1)} %constant_dynamic-update-slice_fusion.refs_0_, bf16[384,768]{1,0:T(8,128)(2,1)S(1)} %constant_dynamic-update-slice_fusion.4.refs_1_, bf16[256,768]{1,0:T(8,128)(2,1)S(1)} %collective-permute-done.7.refs_2_.refs_3_, ...), custom_call_target="tpu_custom_call" | custom-call | flops 704643072 | bytes 2162688 | tf_op jit(solution)/shard_map/pallas_call | solution.py:234
  37.0 0.0 collective-permute-done.6.refs_2_
  37.1 0.1 collective-permute-start.9
  37.2 0.0 collective-permute-done.10.refs_5_
  37.2 1.3 %shard_map.33.refs_4_ = f32[8,128]{1,0:T(8,128)S(1)} custom-call(bf16[512,768]{1,0:T(8,128)(2,1)S(1)} %constant_dynamic-update-slice_fusion.refs_0_, bf16[384,768]{1,0:T(8,128)(2,1)S(1)} %constant_dynamic-update-slice_fusion.4.refs_1_, bf16[128,768]{1,0:T(8,128)(2,1)S(1)} %collective-permute-done.6.refs_2_, ...), custom_call_target="tpu_custom_call" | custom-call | flops 679477248 | bytes 2752512 | tf_op jit(solution)/shard_map/pallas_call | solution.py:234
  38.5 0.4 collective-permute-done.9.refs_3_
  38.9 0.8 %shard_map.34 = f32[8,128]{1,0:T(8,128)S(1)} custom-call(bf16[512,768]{1,0:T(8,128)(2,1)S(1)} %constant_dynamic-update-slice_fusion.refs_0_, bf16[384,768]{1,0:T(8,128)(2,1)S(1)} %constant_dynamic-update-slice_fusion.4.refs_1_, bf16[128,768]{1,0:T(8,128)(2,1)S(1)} %collective-permute-done.6.refs_2_, bf16[256,768]{1,0:T(8,128)(2,1)S(1)} %collective-permute-done.9.refs_3_, ...), custom_call_target="tpu_custom_call" | custom-call | flops 603979776 | bytes 1966080 | tf_op jit(solution)/shard_map/pallas_call | solution.py:234
  39.7 14.8 %all_to_all.11 = f32[8,1,128]{2,1,0:T(1,128)S(1)} all-to-all(f32[8,1,128]{2,1,0:T(1,128)S(1)} %bitcast.5), channel_id=1, replica_groups={{0,2,4,6,8,10,12,14},{1,3,5,7,9,11,13,15},{16,18,20,22,24,26,28,30},{17..., dimensions={0} | all-to-all | bytes 8192 | tf_op jit(solution)/shard_map/all_to_all | solution.py:333
  54.5 0.8 %shard_map.35 = f32[768]{0:T(1024)} custom-call(s32[1,768]{1,0:T(1,128)S(1)} %get-tuple-element.19.slot_ref, f32[8,128]{1,0:T(8,128)S(1)} %bitcast.4), custom_call_target="tpu_custom_call" | custom-call | tf_op jit(solution)/shard_map/pallas_call | solution.py:270
  (11 shorter events, 0.2 us)
Async XLA Ops:
  2.2 18.4 %collective-permute-start = (bf16[128,768]{1,0:T(8,128)(2,1)S(1)}, bf16[128,768]{1,0:T(8,128)(2,1)S(1)}, u32[]{:S(2)}, u32[]{:S(2)}) collective-permute-start(bf16[128,768]{1,0:T(8,128)(2,1)S(1)} %get-tuple-element.23), channel_id=1, source_target_pairs={{0,8},{1,9},{2,10},{3,11},{4,12},{5,13},{6,14},{7,15},{8,0},{9,1},... | collective-permute-start | bytes 589832 | tf_op jit(solution)/shard_map/ppermute | solution.py:280
  6.3 20.6 %collective-permute-start.1 = (bf16[128,768]{1,0:T(8,128)(2,1)S(1)}, bf16[128,768]{1,0:T(8,128)(2,1)S(1)}, u32[]{:S(2)}, u32[]{:S(2)}) collective-permute-start(bf16[128,768]{1,0:T(8,128)(2,1)S(1)} %get-tuple-element.24), channel_id=1, source_target_pairs={{0,10},{1,11},{2,8},{3,9},{4,14},{5,15},{6,12},{7,13},{8,2},{9,3},... | collective-permute-start | bytes 589832 | tf_op jit(solution)/shard_map/ppermute | solution.py:280
  8.7 18.2 %collective-permute-start.2 = (bf16[128,768]{1,0:T(8,128)(2,1)S(1)}, bf16[128,768]{1,0:T(8,128)(2,1)S(1)}, u32[]{:S(2)}, u32[]{:S(2)}) collective-permute-start(bf16[128,768]{1,0:T(8,128)(2,1)S(1)} %get-tuple-element.25), channel_id=1, source_target_pairs={{0,2},{1,3},{2,0},{3,1},{4,6},{5,7},{6,4},{7,5},{8,10},{9,11},{10,... | collective-permute-start | bytes 589832 | tf_op jit(solution)/shard_map/ppermute | solution.py:280
  9.0 20.3 %collective-permute-start.3 = (bf16[128,768]{1,0:T(8,128)(2,1)S(1)}, bf16[128,768]{1,0:T(8,128)(2,1)S(1)}, u32[]{:S(2)}, u32[]{:S(2)}) collective-permute-start(bf16[128,768]{1,0:T(8,128)(2,1)S(1)} %get-tuple-element.26), channel_id=1, source_target_pairs={{0,4},{1,5},{2,6},{3,7},{4,0},{5,1},{6,2},{7,3},{8,12},{9,13},{10,... | collective-permute-start | bytes 589832 | tf_op jit(solution)/shard_map/ppermute | solution.py:280
  10.9 23.1 %collective-permute-start.4 = (bf16[128,768]{1,0:T(8,128)(2,1)S(1)}, bf16[128,768]{1,0:T(8,128)(2,1)S(1)}, u32[]{:S(2)}, u32[]{:S(2)}) collective-permute-start(bf16[128,768]{1,0:T(8,128)(2,1)S(1)} %get-tuple-element.27), channel_id=1, source_target_pairs={{0,6},{1,7},{2,4},{3,5},{4,2},{5,3},{6,0},{7,1},{8,14},{9,15},{10,... | collective-permute-start | bytes 589832 | tf_op jit(solution)/shard_map/ppermute | solution.py:280
  20.6 14.1 %collective-permute-start.5 = (bf16[128,768]{1,0:T(8,128)(2,1)S(1)}, bf16[128,768]{1,0:T(8,128)(2,1)S(1)}, u32[]{:S(2)}, u32[]{:S(2)}) collective-permute-start(bf16[128,768]{1,0:T(8,128)(2,1)S(1)} %get-tuple-element.29), channel_id=1, source_target_pairs={{0,12},{1,13},{2,14},{3,15},{4,8},{5,9},{6,10},{7,11},{8,4},{9,5},... | collective-permute-start | bytes 589832 | tf_op jit(solution)/shard_map/ppermute | solution.py:280
  27.6 9.5 %collective-permute-start.6 = (bf16[128,768]{1,0:T(8,128)(2,1)S(1)}, bf16[128,768]{1,0:T(8,128)(2,1)S(1)}, u32[]{:S(2)}, u32[]{:S(2)}) collective-permute-start(bf16[128,768]{1,0:T(8,128)(2,1)S(1)} %get-tuple-element.31), channel_id=1, source_target_pairs={{0,14},{1,15},{2,12},{3,13},{4,10},{5,11},{6,8},{7,9},{8,6},{9,7},... | collective-permute-start | bytes 589832 | tf_op jit(solution)/shard_map/ppermute | solution.py:280
  29.2 6.8 %collective-permute-start.7 = (bf16[256,768]{1,0:T(8,128)(2,1)S(1)}, bf16[256,768]{1,0:T(8,128)(2,1)S(1)}, u32[]{:S(2)}, u32[]{:S(2)}) collective-permute-start(bf16[256,768]{1,0:T(8,128)(2,1)S(1)} %pad_maximum_fusion), channel_id=1, source_target_pairs={{0,1},{1,0},{2,3},{3,2},{4,5},{5,4},{6,7},{7,6},{8,9},{9,8},{10,11... | collective-permute-start | bytes 1179656 | tf_op jit(solution)/shard_map/ppermute | solution.py:280
  34.0 2.0 %collective-permute-start.8 = (bf16[256,768]{1,0:T(8,128)(2,1)S(1)}, bf16[256,768]{1,0:T(8,128)(2,1)S(1)}, u32[]{:S(2)}, u32[]{:S(2)}) collective-permute-start(bf16[256,768]{1,0:T(8,128)(2,1)S(1)} %pad_maximum_fusion.1), channel_id=1, source_target_pairs={{0,1},{1,0},{2,3},{3,2},{4,5},{5,4},{6,7},{7,6},{8,9},{9,8},{10,11... | collective-permute-start | bytes 1179656 | tf_op jit(solution)/shard_map/ppermute | solution.py:280
  34.1 3.1 %collective-permute-start.10 = (bf16[256,768]{1,0:T(8,128)(2,1)S(1)}, bf16[256,768]{1,0:T(8,128)(2,1)S(1)}, u32[]{:S(2)}, u32[]{:S(2)}) collective-permute-start(bf16[256,768]{1,0:T(8,128)(2,1)S(1)} %pad_maximum_fusion.3), channel_id=1, source_target_pairs={{0,1},{1,0},{2,3},{3,2},{4,5},{5,4},{6,7},{7,6},{8,9},{9,8},{10,11... | collective-permute-start | bytes 1179656 | tf_op jit(solution)/shard_map/ppermute | solution.py:280
  37.1 1.8 %collective-permute-start.9 = (bf16[256,768]{1,0:T(8,128)(2,1)S(1)}, bf16[256,768]{1,0:T(8,128)(2,1)S(1)}, u32[]{:S(2)}, u32[]{:S(2)}) collective-permute-start(bf16[256,768]{1,0:T(8,128)(2,1)S(1)} %pad_maximum_fusion.2), channel_id=1, source_target_pairs={{0,1},{1,0},{2,3},{3,2},{4,5},{5,4},{6,7},{7,6},{8,9},{9,8},{10,11... | collective-permute-start | bytes 1179656 | tf_op jit(solution)/shard_map/ppermute | solution.py:280

commit v6 on v5

--- a/solution.py
+++ b/solution.py
@@ -312,10 +312,10 @@
         best = score([early, mid], [((0,), [1], True), ((1,), [0, 1], False)], best)
         best = score([early, mid, first_other, near_other], [((0, 1), [2, 3], True)], best)
         late = have[7] = after(have[7], best)
-        late_other = swap(join(6, 7))
+        six_other, late_other = swap(have[6]), swap(late)
         best = score(
-            [early, mid, late, first_other, near_other, second_other],
-            [((0, 1), [5], True), ((2,), [0, 1, 3, 4, 5], False)],
+            [early, mid, late, first_other, near_other, second_other, six_other],
+            [((0, 1), [5, 6], True), ((2,), [0, 1, 3, 4, 5, 6], False)],
             best,
         )
         best = score(

time: 55.5 us -> 55.1 us (level)
  blocking collectives: 14.8 us -> 14.2 us
  starting transfers between devices: 14.1 us -> 14.7 us
    all_to_all x1, blocking collectives: 14.8 us -> 14.2 us  [on_device(): lax.all_to_all(best, 'owners', 0, 0, axis_index_groups=same_core, tiled=T...]
    ppermute x11 -> x12, starting transfers between devices: 14.1 us -> 14.7 us  [by_xor(): lax.ppermute(value, axis, [(source, source ^ mask) for source in range(la...]
    ppermute x11 -> x12, waiting for transfers between devices: 16.8 us -> 16.4 us  [by_xor(): lax.ppermute(value, axis, [(source, source ^ mask) for source in range(la...]
  transfers between devices with their start and end apart: 11 -> 12, of which waited for: 4 -> 3; matrix products, arithmetic and copies ran while one was open for 0% -> 0% of each run, Pallas kernels for 10% -> 10%
where the time goes in v6:
time: 55.1 us; the launch traced here: 54.9 us
  waiting for transfers between devices  16.4 us (30%)
  starting transfers between devices  14.7 us (27%)
  blocking collectives  14.2 us (26%)
  Pallas kernels  9.21 us (17%)
    ppermute x12, waiting for transfers between devices, by_xor(): lax.ppermute(value, axis, [(source, source ^ mask) for source in range(la...  16.4 us
    ppermute x12, starting transfers between devices, by_xor(): lax.ppermute(value, axis, [(source, source ^ mask) for source in range(la...  14.7 us
    all_to_all x1, blocking collectives, on_device(): lax.all_to_all(best, 'owners', 0, 0, axis_index_groups=same_core, tiled=T...  14.2 us
    pallas_call x5, Pallas kernels, score(): pl.pallas_call(functools.partial(score_kernel, plan, len(blocks), start i...  5.09 us
    pallas_call x1, Pallas kernels, pack(): pl.pallas_call(functools.partial(pack_kernel, taken, mixed, clusters, cap...  2.21 us
    pallas_call x1, Pallas kernels, pack_more(): pl.pallas_call(functools.partial(more_kernel, taken, capacity), in_specs=...  1.11 us
  transfers between devices with their start and end apart: 12, of which 3 were waited for; matrix products, arithmetic and copies ran while one was open for 0% of the time, Pallas kernels for 10%

profile of v6, /device:TPU:0, one launch (start us, length us, event | category | flops | bytes accessed | tf_op | source)
XLA Modules:
  0.0 54.9 jit_solution(10518609624529273600)
XLA Ops:
  0.0 2.2 %shard_map.28 = (bf16[128,768]{1,0:T(8,128)(2,1)S(1)}, bf16[128,768]{1,0:T(8,128)(2,1)S(1)}, s32[1,768]{1,0:T(1,128)S(1)}, f32[8,128]{1,0:T(8,128)S(1)}, bf16[768,768]{1,0:T(8,128)(2,1)S(1)}) custom-call(s32[768]{0:T(1024)} %cluster_ref.1, f32[768,768]{1,0:T(8,128)} %rows_ref.1), custom_call_target="tpu_custom_call" | custom-call | flops 301989888 | bytes 2752512 | tf_op jit(solution)/shard_map/pallas_call | solution.py:107
  2.2 4.1 %collective-permute-start = (bf16[128,768]{1,0:T(8,128)(2,1)S(1)}, bf16[128,768]{1,0:T(8,128)(2,1)S(1)}, u32[]{:S(2)}, u32[]{:S(2)}) collective-permute-start(bf16[128,768]{1,0:T(8,128)(2,1)S(1)} %get-tuple-element.23), channel_id=1, source_target_pairs={{0,8},{1,9},{2,10},{3,11},{4,12},{5,13},{6,14},{7,15},{8,0},{9,1},... | collective-permute-start | bytes 589832 | tf_op jit(solution)/shard_map/ppermute | solution.py:280
  6.3 1.3 %collective-permute-start.1 = (bf16[128,768]{1,0:T(8,128)(2,1)S(1)}, bf16[128,768]{1,0:T(8,128)(2,1)S(1)}, u32[]{:S(2)}, u32[]{:S(2)}) collective-permute-start(bf16[128,768]{1,0:T(8,128)(2,1)S(1)} %get-tuple-element.24), channel_id=1, source_target_pairs={{0,10},{1,11},{2,8},{3,9},{4,14},{5,15},{6,12},{7,13},{8,2},{9,3},... | collective-permute-start | bytes 589832 | tf_op jit(solution)/shard_map/ppermute | solution.py:280
  7.6 1.1 %shard_map.29 = (bf16[128,768]{1,0:T(8,128)(2,1)S(1)}, bf16[128,768]{1,0:T(8,128)(2,1)S(1)}, bf16[128,768]{1,0:T(8,128)(2,1)S(1)}, bf16[128,768]{1,0:T(8,128)(2,...) custom-call(s32[1,768]{1,0:T(1,128)S(1)} %get-tuple-element.19.slot_ref, ...), custom_call_target="tpu_custom_call" | custom-call | flops 905969664 | bytes 3538944 | tf_op jit(solution)/shard_map/pallas_call | solution.py:142
  8.7 0.3 collective-permute-start.2
  9.1 1.8 %collective-permute-start.3 = (bf16[128,768]{1,0:T(8,128)(2,1)S(1)}, bf16[128,768]{1,0:T(8,128)(2,1)S(1)}, u32[]{:S(2)}, u32[]{:S(2)}) collective-permute-start(bf16[128,768]{1,0:T(8,128)(2,1)S(1)} %get-tuple-element.26), channel_id=1, source_target_pairs={{0,4},{1,5},{2,6},{3,7},{4,0},{5,1},{6,2},{7,3},{8,12},{9,13},{10,... | collective-permute-start | bytes 589832 | tf_op jit(solution)/shard_map/ppermute | solution.py:280
  10.9 1.4 %collective-permute-start.4 = (bf16[128,768]{1,0:T(8,128)(2,1)S(1)}, bf16[128,768]{1,0:T(8,128)(2,1)S(1)}, u32[]{:S(2)}, u32[]{:S(2)}) collective-permute-start(bf16[128,768]{1,0:T(8,128)(2,1)S(1)} %get-tuple-element.27), channel_id=1, source_target_pairs={{0,6},{1,7},{2,4},{3,5},{4,2},{5,3},{6,0},{7,1},{8,14},{9,15},{10,... | collective-permute-start | bytes 589832 | tf_op jit(solution)/shard_map/ppermute | solution.py:280
  12.3 8.3 %collective-permute-done = bf16[128,768]{1,0:T(8,128)(2,1)S(1)} collective-permute-done((bf16[128,768]{1,0:T(8,128)(2,1)S(1)}, bf16[128,768]{1,0:T(8,128)(2,1)S(1)}, u32[]{:S(2)}, u32[]{:S(2)}) %collective-permute-start) | collective-permute-done | bytes 196640 | tf_op jit(solution)/shard_map/ppermute | solution.py:280
  20.6 2.8 %collective-permute-start.5 = (bf16[128,768]{1,0:T(8,128)(2,1)S(1)}, bf16[128,768]{1,0:T(8,128)(2,1)S(1)}, u32[]{:S(2)}, u32[]{:S(2)}) collective-permute-start(bf16[128,768]{1,0:T(8,128)(2,1)S(1)} %get-tuple-element.29), channel_id=1, source_target_pairs={{0,12},{1,13},{2,14},{3,15},{4,8},{5,9},{6,10},{7,11},{8,4},{9,5},... | collective-permute-start | bytes 589832 | tf_op jit(solution)/shard_map/ppermute | solution.py:280
  23.4 3.5 %collective-permute-done.1 = bf16[128,768]{1,0:T(8,128)(2,1)S(1)} collective-permute-done((bf16[128,768]{1,0:T(8,128)(2,1)S(1)}, bf16[128,768]{1,0:T(8,128)(2,1)S(1)}, u32[]{:S(2)}, u32[]{:S(2)}) %collective-permute-start.1) | collective-permute-done | bytes 196640 | tf_op jit(solution)/shard_map/ppermute | solution.py:280
  26.9 0.0 collective-permute-done.2
  27.0 0.6 %shard_map.30.refs_2_ = f32[4,128]{1,0:T(4,128)S(1)} custom-call(bf16[512,768]{1,0:T(8,128)(2,1)S(1)} %constant_dynamic-update-slice_fusion.refs_0_), custom_call_target="tpu_custom_call" | custom-call | flops 402653184 | bytes 786432 | tf_op jit(solution)/shard_map/pallas_call | solution.py:234
  27.6 1.6 %collective-permute-start.6 = (bf16[128,768]{1,0:T(8,128)(2,1)S(1)}, bf16[128,768]{1,0:T(8,128)(2,1)S(1)}, u32[]{:S(2)}, u32[]{:S(2)}) collective-permute-start(bf16[128,768]{1,0:T(8,128)(2,1)S(1)} %get-tuple-element.31), channel_id=1, source_target_pairs={{0,14},{1,15},{2,12},{3,13},{4,10},{5,11},{6,8},{7,9},{8,6},{9,7},... | collective-permute-start | bytes 589832 | tf_op jit(solution)/shard_map/ppermute | solution.py:280
  29.2 0.1 collective-permute-start.7
  29.3 0.0 collective-permute-done.3
  29.3 4.6 %collective-permute-done.4 = bf16[128,768]{1,0:T(8,128)(2,1)S(1)} collective-permute-done((bf16[128,768]{1,0:T(8,128)(2,1)S(1)}, bf16[128,768]{1,0:T(8,128)(2,1)S(1)}, u32[]{:S(2)}, u32[]{:S(2)}) %collective-permute-start.4) | collective-permute-done | bytes 196640 | tf_op jit(solution)/shard_map/ppermute | solution.py:280
  34.0 0.1 collective-permute-start.8
  34.1 0.6 %collective-permute-start.10 = (bf16[256,768]{1,0:T(8,128)(2,1)S(1)}, bf16[256,768]{1,0:T(8,128)(2,1)S(1)}, u32[]{:S(2)}, u32[]{:S(2)}) collective-permute-start(bf16[256,768]{1,0:T(8,128)(2,1)S(1)} %pad_maximum_fusion.2), channel_id=1, source_target_pairs={{0,1},{1,0},{2,3},{3,2},{4,5},{5,4},{6,7},{7,6},{8,9},{9,8},{10,11... | collective-permute-start | bytes 1179656 | tf_op jit(solution)/shard_map/ppermute | solution.py:280
  34.7 0.0 collective-permute-done.5
  34.7 0.1 collective-permute-start.11
  34.8 1.3 %shard_map.31.refs_4_ = f32[7,128]{1,0:T(8,128)S(1)} custom-call(bf16[512,768]{1,0:T(8,128)(2,1)S(1)} %constant_dynamic-update-slice_fusion.refs_0_, bf16[384,768]{1,0:T(8,128)(2,1)S(1)} %constant_dynamic-update-slice_fusion.4.refs_1_, f32[4,128]{1,0:T(4,128)S(1)} %shard_map.30.refs_2_), custom_call_target="tpu_custom_call" | custom-call | flops 830472192 | bytes 1376256 | tf_op jit(solution)/shard_map/pallas_call | solution.py:234
  36.1 0.0 collective-permute-done.7.refs_2_.refs_3_
  36.1 0.0 collective-permute-done.8.refs_3_.refs_4_
  36.1 1.0 %shard_map.32.refs_7_ = f32[7,128]{1,0:T(8,128)S(1)} custom-call(bf16[512,768]{1,0:T(8,128)(2,1)S(1)} %constant_dynamic-update-slice_fusion.refs_0_, bf16[384,768]{1,0:T(8,128)(2,1)S(1)} %constant_dynamic-update-slice_fusion.4.refs_1_, bf16[256,768]{1,0:T(8,128)(2,1)S(1)} %collective-permute-done.7.refs_2_.refs_3_, ...), custom_call_target="tpu_custom_call" | custom-call | flops 704643072 | bytes 2162688 | tf_op jit(solution)/shard_map/pallas_call | solution.py:234
  37.1 0.0 collective-permute-done.6.refs_2_
  37.1 0.6 %collective-permute-start.9 = (bf16[128,768]{1,0:T(8,128)(2,1)S(1)}, bf16[128,768]{1,0:T(8,128)(2,1)S(1)}, u32[]{:S(2)}, u32[]{:S(2)}) collective-permute-start(bf16[128,768]{1,0:T(8,128)(2,1)S(1)} %collective-permute-done.6.refs_2_), channel_id=1, source_target_pairs={{0,1},{1,0},{2,3},{3,2},{4,5},{5,4},{6,7},{7,6},{8,9},{9,8},{10,11... | collective-permute-start | bytes 589832 | tf_op jit(solution)/shard_map/ppermute | solution.py:280
  37.7 0.0 collective-permute-done.10.refs_5_
  37.7 0.0 collective-permute-done.11.refs_6_
  37.7 1.6 %shard_map.33.refs_4_ = f32[8,128]{1,0:T(8,128)S(1)} custom-call(bf16[512,768]{1,0:T(8,128)(2,1)S(1)} %constant_dynamic-update-slice_fusion.refs_0_, bf16[384,768]{1,0:T(8,128)(2,1)S(1)} %constant_dynamic-update-slice_fusion.4.refs_1_, bf16[128,768]{1,0:T(8,128)(2,1)S(1)} %collective-permute-done.6.refs_2_, ...), custom_call_target="tpu_custom_call" | custom-call | flops 880803840 | bytes 2949120 | tf_op jit(solution)/shard_map/pallas_call | solution.py:234
  39.3 0.0 collective-permute-done.9.refs_3_
  39.3 0.6 %shard_map.34 = f32[8,128]{1,0:T(8,128)S(1)} custom-call(bf16[512,768]{1,0:T(8,128)(2,1)S(1)} %constant_dynamic-update-slice_fusion.refs_0_, bf16[384,768]{1,0:T(8,128)(2,1)S(1)} %constant_dynamic-update-slice_fusion.4.refs_1_, bf16[128,768]{1,0:T(8,128)(2,1)S(1)} %collective-permute-done.6.refs_2_, bf16[128,768]{1,0:T(8,128)(2,1)S(1)} %collective-permute-done.9.refs_3_, ...), custom_call_target="tpu_custom_call" | custom-call | flops 402653184 | bytes 1769472 | tf_op jit(solution)/shard_map/pallas_call | solution.py:234
  39.9 14.2 %all_to_all.11 = f32[8,1,128]{2,1,0:T(1,128)S(1)} all-to-all(f32[8,1,128]{2,1,0:T(1,128)S(1)} %bitcast.4), channel_id=1, replica_groups={{0,2,4,6,8,10,12,14},{1,3,5,7,9,11,13,15},{16,18,20,22,24,26,28,30},{17..., dimensions={0} | all-to-all | bytes 8192 | tf_op jit(solution)/shard_map/all_to_all | solution.py:333
  54.1 0.8 %shard_map.35 = f32[768]{0:T(1024)} custom-call(s32[1,768]{1,0:T(1,128)S(1)} %get-tuple-element.19.slot_ref, f32[8,128]{1,0:T(8,128)S(1)} %bitcast.5), custom_call_target="tpu_custom_call" | custom-call | tf_op jit(solution)/shard_map/pallas_call | solution.py:270
  (10 shorter events, 0.2 us)
Async XLA Ops:
  2.2 18.4 %collective-permute-start = (bf16[128,768]{1,0:T(8,128)(2,1)S(1)}, bf16[128,768]{1,0:T(8,128)(2,1)S(1)}, u32[]{:S(2)}, u32[]{:S(2)}) collective-permute-start(bf16[128,768]{1,0:T(8,128)(2,1)S(1)} %get-tuple-element.23), channel_id=1, source_target_pairs={{0,8},{1,9},{2,10},{3,11},{4,12},{5,13},{6,14},{7,15},{8,0},{9,1},... | collective-permute-start | bytes 589832 | tf_op jit(solution)/shard_map/ppermute | solution.py:280
  6.3 20.6 %collective-permute-start.1 = (bf16[128,768]{1,0:T(8,128)(2,1)S(1)}, bf16[128,768]{1,0:T(8,128)(2,1)S(1)}, u32[]{:S(2)}, u32[]{:S(2)}) collective-permute-start(bf16[128,768]{1,0:T(8,128)(2,1)S(1)} %get-tuple-element.24), channel_id=1, source_target_pairs={{0,10},{1,11},{2,8},{3,9},{4,14},{5,15},{6,12},{7,13},{8,2},{9,3},... | collective-permute-start | bytes 589832 | tf_op jit(solution)/shard_map/ppermute | solution.py:280
  8.7 18.2 %collective-permute-start.2 = (bf16[128,768]{1,0:T(8,128)(2,1)S(1)}, bf16[128,768]{1,0:T(8,128)(2,1)S(1)}, u32[]{:S(2)}, u32[]{:S(2)}) collective-permute-start(bf16[128,768]{1,0:T(8,128)(2,1)S(1)} %get-tuple-element.25), channel_id=1, source_target_pairs={{0,2},{1,3},{2,0},{3,1},{4,6},{5,7},{6,4},{7,5},{8,10},{9,11},{10,... | collective-permute-start | bytes 589832 | tf_op jit(solution)/shard_map/ppermute | solution.py:280
  9.1 20.2 %collective-permute-start.3 = (bf16[128,768]{1,0:T(8,128)(2,1)S(1)}, bf16[128,768]{1,0:T(8,128)(2,1)S(1)}, u32[]{:S(2)}, u32[]{:S(2)}) collective-permute-start(bf16[128,768]{1,0:T(8,128)(2,1)S(1)} %get-tuple-element.26), channel_id=1, source_target_pairs={{0,4},{1,5},{2,6},{3,7},{4,0},{5,1},{6,2},{7,3},{8,12},{9,13},{10,... | collective-permute-start | bytes 589832 | tf_op jit(solution)/shard_map/ppermute | solution.py:280
  10.9 23.1 %collective-permute-start.4 = (bf16[128,768]{1,0:T(8,128)(2,1)S(1)}, bf16[128,768]{1,0:T(8,128)(2,1)S(1)}, u32[]{:S(2)}, u32[]{:S(2)}) collective-permute-start(bf16[128,768]{1,0:T(8,128)(2,1)S(1)} %get-tuple-element.27), channel_id=1, source_target_pairs={{0,6},{1,7},{2,4},{3,5},{4,2},{5,3},{6,0},{7,1},{8,14},{9,15},{10,... | collective-permute-start | bytes 589832 | tf_op jit(solution)/shard_map/ppermute | solution.py:280
  20.6 14.1 %collective-permute-start.5 = (bf16[128,768]{1,0:T(8,128)(2,1)S(1)}, bf16[128,768]{1,0:T(8,128)(2,1)S(1)}, u32[]{:S(2)}, u32[]{:S(2)}) collective-permute-start(bf16[128,768]{1,0:T(8,128)(2,1)S(1)} %get-tuple-element.29), channel_id=1, source_target_pairs={{0,12},{1,13},{2,14},{3,15},{4,8},{5,9},{6,10},{7,11},{8,4},{9,5},... | collective-permute-start | bytes 589832 | tf_op jit(solution)/shard_map/ppermute | solution.py:280
  27.6 9.5 %collective-permute-start.6 = (bf16[128,768]{1,0:T(8,128)(2,1)S(1)}, bf16[128,768]{1,0:T(8,128)(2,1)S(1)}, u32[]{:S(2)}, u32[]{:S(2)}) collective-permute-start(bf16[128,768]{1,0:T(8,128)(2,1)S(1)} %get-tuple-element.31), channel_id=1, source_target_pairs={{0,14},{1,15},{2,12},{3,13},{4,10},{5,11},{6,8},{7,9},{8,6},{9,7},... | collective-permute-start | bytes 589832 | tf_op jit(solution)/shard_map/ppermute | solution.py:280
  29.2 6.9 %collective-permute-start.7 = (bf16[256,768]{1,0:T(8,128)(2,1)S(1)}, bf16[256,768]{1,0:T(8,128)(2,1)S(1)}, u32[]{:S(2)}, u32[]{:S(2)}) collective-permute-start(bf16[256,768]{1,0:T(8,128)(2,1)S(1)} %pad_maximum_fusion), channel_id=1, source_target_pairs={{0,1},{1,0},{2,3},{3,2},{4,5},{5,4},{6,7},{7,6},{8,9},{9,8},{10,11... | collective-permute-start | bytes 1179656 | tf_op jit(solution)/shard_map/ppermute | solution.py:280
  34.0 2.1 %collective-permute-start.8 = (bf16[256,768]{1,0:T(8,128)(2,1)S(1)}, bf16[256,768]{1,0:T(8,128)(2,1)S(1)}, u32[]{:S(2)}, u32[]{:S(2)}) collective-permute-start(bf16[256,768]{1,0:T(8,128)(2,1)S(1)} %pad_maximum_fusion.1), channel_id=1, source_target_pairs={{0,1},{1,0},{2,3},{3,2},{4,5},{5,4},{6,7},{7,6},{8,9},{9,8},{10,11... | collective-permute-start | bytes 1179656 | tf_op jit(solution)/shard_map/ppermute | solution.py:280
  34.1 3.6 %collective-permute-start.10 = (bf16[256,768]{1,0:T(8,128)(2,1)S(1)}, bf16[256,768]{1,0:T(8,128)(2,1)S(1)}, u32[]{:S(2)}, u32[]{:S(2)}) collective-permute-start(bf16[256,768]{1,0:T(8,128)(2,1)S(1)} %pad_maximum_fusion.2), channel_id=1, source_target_pairs={{0,1},{1,0},{2,3},{3,2},{4,5},{5,4},{6,7},{7,6},{8,9},{9,8},{10,11... | collective-permute-start | bytes 1179656 | tf_op jit(solution)/shard_map/ppermute | solution.py:280
  34.7 3.0 %collective-permute-start.11 = (bf16[128,768]{1,0:T(8,128)(2,1)S(1)}, bf16[128,768]{1,0:T(8,128)(2,1)S(1)}, u32[]{:S(2)}, u32[]{:S(2)}) collective-permute-start(bf16[128,768]{1,0:T(8,128)(2,1)S(1)} %collective-permute-done.5), channel_id=1, source_target_pairs={{0,1},{1,0},{2,3},{3,2},{4,5},{5,4},{6,7},{7,6},{8,9},{9,8},{10,11... | collective-permute-start | bytes 589832 | tf_op jit(solution)/shard_map/ppermute | solution.py:280
  37.1 2.1 %collective-permute-start.9 = (bf16[128,768]{1,0:T(8,128)(2,1)S(1)}, bf16[128,768]{1,0:T(8,128)(2,1)S(1)}, u32[]{:S(2)}, u32[]{:S(2)}) collective-permute-start(bf16[128,768]{1,0:T(8,128)(2,1)S(1)} %collective-permute-done.6.refs_2_), channel_id=1, source_target_pairs={{0,1},{1,0},{2,3},{3,2},{4,5},{5,4},{6,7},{7,6},{8,9},{9,8},{10,11... | collective-permute-start | bytes 589832 | tf_op jit(solution)/shard_map/ppermute | solution.py:280
